TPU v7x, 32 devices: a whole 2x2x4 slice. The times are simulated.
32 devices in a mesh: atom: 8 (over z, x), chan: 2 (over core), rep: 2 (over y).
Axes of the slice: x: 2, y: 2, z: 4, core: 2. Of those that a mesh axis runs over, the one named last changes fastest.
Arguments:
- feats: bfloat16 [2, 128, 81, 128], P('rep', 'chan', None, 'atom'), may hold values from -6 to 6
- neighbors: int32 [2, 128, 32], P('rep', 'atom'), may hold values from 0 to 127, as said below
- counts: int32 [2, 128], P('rep', 'atom'), may hold values from 1 to 32, as said below
- radial: bfloat16 [2, 8, 4096], P('rep', None, 'atom'), may hold values from 2 to 6
- filter_weight: bfloat16 [8, 128, 81], P(None, 'chan'), may hold values from -0.3125 to 0.3125
- message_grad: bfloat16 [2, 128, 81, 4096], P('rep', 'chan', None, 'atom'), may hold values from -2 to 2
Outputs:
- feat_grad: float32 [2, 128, 81, 128], P('rep', 'chan', None, 'atom')
- radial_grad: float32 [2, 8, 4096], P('rep', None, 'atom')
- weight_grad: float32 [8, 128, 81], P(None, 'chan')
Inputs may be any that keep to these rules, and one draw needn't show every extreme that they name: `neighbors`: each source atom lies, counted cyclically, in the block of 16 consecutive atoms that holds its receiver or in one of the 2 such blocks on either side. `counts`: some atom of every crystal has all 32 slots valid.
All inputs are finite; a program needn't handle non-finite values.
Results may differ from a plain program's by a relative error of at most 0.0054.
Values may be sent and summed in bfloat16 or wider, within the bound.
A program may use at most 64 MiB of HBM per device.

v0:
```python
import jax
import jax.numpy as jnp
from jax import lax
from jax.sharding import PartitionSpec as P

BASIS = 9
POINTS = 16
SLOTS = 32
REACH = 2
G = 81
SAMPLES = 256


def passed_along(value, axis, steps):
    count = lax.axis_size(axis)
    pairs = [(source, (source + steps) % count) for source in range(count)]
    return lax.ppermute(value, axis, pairs)


def basis_table():
    points = jnp.arange(POINTS, dtype=jnp.float32) * jnp.float32(2.0 * 3.141592653589793 / POINTS)
    degree_index = jnp.arange(BASIS, dtype=jnp.int32)
    frequency = ((degree_index + 1) // 2).astype(jnp.float32)
    angles = frequency[:, None] * points[None, :]
    root_two = jnp.sqrt(jnp.float32(2.0))
    single = jnp.where(
        degree_index[:, None] == 0,
        jnp.ones_like(angles),
        jnp.where(
            degree_index[:, None] % 2 == 1, root_two * jnp.cos(angles), root_two * jnp.sin(angles)
        ),
    )
    product = single[:, None, :, None] * single[None, :, None, :]
    return product.reshape(G, SAMPLES).astype(jnp.bfloat16)


def channel_terms(gathered, grad_c, weight_c, radial_e, valid_mask, synth_table, synth_rows):
    filter_edge = jnp.dot(weight_c.T, radial_e, preferred_element_type=jnp.float32).astype(
        jnp.bfloat16
    )
    feat_grid = jnp.dot(synth_rows, gathered, preferred_element_type=jnp.float32)
    filt_grid = jnp.dot(synth_rows, filter_edge, preferred_element_type=jnp.float32)
    weighted = (
        jnp.dot(synth_rows, grad_c, preferred_element_type=jnp.float32)
        * (valid_mask / SAMPLES)[None, :]
    )
    feat_side = (weighted * filt_grid).astype(jnp.bfloat16)
    filt_side = (weighted * feat_grid).astype(jnp.bfloat16)
    edge_grad = jnp.dot(synth_table, feat_side, preferred_element_type=jnp.float32).astype(
        jnp.bfloat16
    )
    filt_grad = jnp.dot(synth_table, filt_side, preferred_element_type=jnp.float32).astype(
        jnp.bfloat16
    )
    radial_part = jnp.dot(weight_c, filt_grad, preferred_element_type=jnp.float32)
    weight_part = jnp.dot(radial_e, filt_grad.T, preferred_element_type=jnp.float32)
    return (edge_grad, radial_part, weight_part)


def local(feats, neighbors, counts, radial, filter_weight, message_grad):
    synth_table = basis_table()
    synth_rows = synth_table.T
    atom_count = lax.axis_size("atom")
    position = lax.axis_index("atom")
    block_len = feats.shape[3]
    own_block = feats[0]
    chan_count = own_block.shape[0]
    pieces = []
    for offset in range(-REACH, REACH + 1):
        if offset == 0:
            pieces.append(own_block)
        else:
            pieces.append(passed_along(own_block, "atom", -offset))
    window = jnp.concatenate(pieces, axis=2)
    window_len = window.shape[2]
    sources = neighbors[0].reshape(-1)
    slot_index = (
        sources // block_len - position + REACH
    ) % atom_count * block_len + sources % block_len
    selector = (slot_index[None, :] == jnp.arange(window_len, dtype=jnp.int32)[:, None]).astype(
        jnp.bfloat16
    )
    gathered = jnp.dot(
        window.reshape(chan_count * G, window_len), selector, preferred_element_type=jnp.float32
    )
    gathered = gathered.astype(jnp.bfloat16).reshape(chan_count, G, -1)
    valid_mask = (
        (jnp.arange(SLOTS, dtype=jnp.int32)[None, :] < counts[0][:, None])
        .reshape(-1)
        .astype(jnp.float32)
    )
    radial_e = radial[0]

    def channel_step(running, inputs):
        gathered_c, grad_c, weight_c = inputs
        edge_grad, radial_part, weight_part = channel_terms(
            gathered_c, grad_c, weight_c, radial_e, valid_mask, synth_table, synth_rows
        )
        return (running + radial_part, (edge_grad, weight_part))

    radial_local, (edge_grads, weight_parts) = lax.scan(
        channel_step,
        jnp.zeros(radial_e.shape, jnp.float32),
        (gathered, message_grad[0], jnp.transpose(filter_weight, (1, 0, 2))),
    )
    window_grad = lax.dot_general(
        edge_grads.reshape(chan_count * G, -1),
        selector,
        (((1,), (1,)), ((), ())),
        preferred_element_type=jnp.float32,
    )

    def block_of(offset):
        return window_grad[:, (offset + REACH) * block_len : (offset + REACH + 1) * block_len]

    returned_sum = block_of(0)
    for direction in (1, -1):
        carried = block_of(direction * REACH)
        for offset in range(REACH - 1, -1, -1):
            arrived = passed_along(carried, "atom", direction)
            if offset > 0:
                carried = arrived + block_of(direction * offset)
            else:
                returned_sum = returned_sum + arrived
    feat_grad = returned_sum.reshape(1, chan_count, G, block_len)
    radial_grad = lax.psum(radial_local, "chan")[None]
    weight_summed = lax.psum(jnp.transpose(weight_parts, (1, 0, 2)), ("atom", "rep"))
    weight_grad = weight_summed / (atom_count * block_len * lax.axis_size("rep"))
    return (feat_grad, radial_grad, weight_grad)


def solution(mesh):
    placed = (
        P("rep", "chan", None, "atom"),
        P("rep", "atom", None),
        P("rep", "atom"),
        P("rep", None, "atom"),
        P(None, "chan", None),
        P("rep", "chan", None, "atom"),
    )
    return jax.shard_map(
        local,
        mesh=mesh,
        in_specs=placed,
        out_specs=(P("rep", "chan", None, "atom"), P("rep", None, "atom"), P(None, "chan", None)),
        check_vma=False,
    )
```

profile of v0, /device:TPU:0, one launch (start us, length us, event | category | flops | bytes accessed | tf_op | source)
XLA Modules:
  0.0 570.3 jit_solution(8755748182621560203)
XLA Ops:
  7.2 3.1 collective-permute-start
  10.3 1.5 collective-permute-start.1
  11.8 3.2 collective-permute-start.2
  17.6 8.0 %copy.26 = bf16[1,64,81,512]{3,2,1,0:T(8,128)(2,1)} copy(bf16[1,64,81,512]{3,1,2,0:T(8,128)(2,1)} %param.13) | data formatting | bytes 10616832 | tf_op args[5]
  27.3 2.7 collective-permute-done.3
  30.6 3.9 convolution_convert_fusion.1
  34.5 7.9 %reshape.260 = bf16[64,81,512]{2,1,0:T(8,128)(2,1)} reshape(bf16[5184,512]{1,0:T(8,128)(2,1)} %convolution_convert_fusion.1) | data formatting | bytes 10616832 | tf_op jit(solution)/shard_map/reshape | solution.py:86
  42.4 390.4 %while.18 = (s32[]{:T(128)}, f32[8,512]{1,0:T(8,128)S(1)}, bf16[64,81,512]{2,1,0:T(8,128)(2,1)}, f32[64,8,81]{2,0,1:T(8,128)}, bf16[64,8,81]{2,1,0:T(8,128)(2,1)...) while((s32[]{:T(128)}, f32[8,512]{1,0:T(8,128)S(1)}, ...), condition=%wide.region_1.2_spmd.clone.clone.clone.clone, body=%wide.region_0.1_spmd.clone.clone.clone.clone.sunk | while | flops 108989952 | bytes 2693995 | solution.py:101
  65.3 1.4 dynamic_update_slice.20
  89.7 1.4 dynamic_update_slice.20
  138.5 1.4 dynamic_update_slice.20
  187.3 1.4 dynamic_update_slice.20
  193.4 1.4 dynamic_update_slice.20
  309.3 1.4 dynamic_update_slice.20
  432.8 7.9 %reshape.261 = bf16[5184,512]{1,0:T(8,128)(2,1)} reshape(bf16[64,81,512]{2,1,0:T(8,128)(2,1)} %get-tuple-element.65) | data formatting | bytes 10616832 | tf_op jit(solution)/shard_map/reshape | solution.py:107
  440.7 4.2 fusion.36
  445.0 1.5 collective-permute-start.4
  446.6 3.2 collective-permute-start.6
  449.8 11.9 %collective-permute-done.4 = f32[5184,16]{0,1:T(8,128)S(1)} collective-permute-done((f32[5184,16]{0,1:T(8,128)S(1)}, f32[5184,16]{0,1:T(8,128)S(1)}, u32[]{:S(2)}, u32[]{:S(2)}) %collective-permute-start.4) | collective-permute-done | bytes 331808 | tf_op jit(solution)/shard_map/ppermute | solution.py:17
  461.7 2.3 collective-permute-done.6
  465.4 4.5 collective-permute-start.7
  469.9 3.9 psum.14
  473.8 86.0 %all-reduce.2.cloned.1.call-done = f32[8,64,81]{2,1,0:T(8,128)} async-done(((f32[8,64,81]{2,1,0:T(8,128)}), f32[8,64,81]{2,1,0:T(8,128)}) %all-reduce.2.cloned.1.call-update) | async-done | bytes 165904 | tf_op jit(solution)/shard_map/psum | solution.py:127
  559.8 1.7 broadcast_multiply_fusion.1
  (807 shorter events, 388.6 us)
Async XLA Ops:
  7.2 552.7 %all-reduce.2.cloned.1.call-start = ((), (), s32[]{:S(2)}) async-start(), calls=%async_computation | async-start | bytes 524288 | tf_op jit(solution)/shard_map/psum | solution.py:127
  7.2 18.6 %collective-permute-start = (bf16[64,81,16]{1,2,0:T(8,128)(2,1)}, bf16[64,81,16]{1,2,0:T(8,128)(2,1)S(1)}, u32[]{:S(2)}, u32[]{:S(2)}) collective-permute-start(bf16[64,81,16]{1,2,0:T(8,128)(2,1)} %bitcast.104), channel_id=1, source_target_pairs={{0,8},{4,12},{8,16},{12,20},{16,24},{20,28},{24,0},{28,4},{1,9},{5... | collective-permute-start | bytes 497672 | tf_op jit(solution)/shard_map/ppermute | solution.py:17
  10.3 16.2 %collective-permute-start.1 = (bf16[64,81,16]{1,2,0:T(8,128)(2,1)}, bf16[64,81,16]{1,2,0:T(8,128)(2,1)S(1)}, u32[]{:S(2)}, u32[]{:S(2)}) collective-permute-start(bf16[64,81,16]{1,2,0:T(8,128)(2,1)} %bitcast.105), channel_id=1, source_target_pairs={{0,4},{4,8},{8,12},{12,16},{16,20},{20,24},{24,28},{28,0},{1,5},{5... | collective-permute-start | bytes 497672 | tf_op jit(solution)/shard_map/ppermute | solution.py:17
  11.8 15.1 %collective-permute-start.2 = (bf16[64,81,16]{1,2,0:T(8,128)(2,1)}, bf16[64,81,16]{1,2,0:T(8,128)(2,1)S(1)}, u32[]{:S(2)}, u32[]{:S(2)}) collective-permute-start(bf16[64,81,16]{1,2,0:T(8,128)(2,1)} %bitcast.106), channel_id=1, source_target_pairs={{0,28},{4,0},{8,4},{12,8},{16,12},{20,16},{24,20},{28,24},{1,29},{... | collective-permute-start | bytes 497672 | tf_op jit(solution)/shard_map/ppermute | solution.py:17
  15.0 15.1 %collective-permute-start.3 = (bf16[64,81,16]{1,2,0:T(8,128)(2,1)}, bf16[64,81,16]{1,2,0:T(8,128)(2,1)S(1)}, u32[]{:S(2)}, u32[]{:S(2)}) collective-permute-start(bf16[64,81,16]{1,2,0:T(8,128)(2,1)} %bitcast.107), channel_id=1, source_target_pairs={{0,24},{4,28},{8,0},{12,4},{16,8},{20,12},{24,16},{28,20},{1,25},{... | collective-permute-start | bytes 497672 | tf_op jit(solution)/shard_map/ppermute | solution.py:17
  16.4 9.2 %copy-start.1 = (bf16[8,64,81]{2,1,0:T(8,128)(2,1)S(1)}, bf16[8,64,81]{2,1,0:T(8,128)(2,1)}, u32[]{:S(2)}) copy-start(bf16[8,64,81]{2,1,0:T(8,128)(2,1)} %param.12) | copy-start | bytes 248836
  34.5 7.9 %copy-start = (bf16[1,8,512]{2,1,0:T(8,128)(2,1)S(1)}, bf16[1,8,512]{2,1,0:T(8,128)(2,1)}, u32[]{:S(2)}) copy-start(bf16[1,8,512]{2,1,0:T(8,128)(2,1)} %param.11) | copy-start | bytes 24580
  34.5 7.9 %copy-start.2 = (s32[1,16]{1,0:T(1,128)S(1)}, s32[1,16]{1,0:T(1,128)}, u32[]{:S(2)}) copy-start(s32[1,16]{1,0:T(1,128)} %param.10) | copy-start | bytes 196
  445.0 16.7 %collective-permute-start.4 = (f32[5184,16]{0,1:T(8,128)S(1)}, f32[5184,16]{0,1:T(8,128)S(1)}, u32[]{:S(2)}, u32[]{:S(2)}) collective-permute-start(f32[5184,16]{0,1:T(8,128)S(1)} %get-tuple-element.219), channel_id=1, source_target_pairs={{0,4},{4,8},{8,12},{12,16},{16,20},{20,24},{24,28},{28,0},{1,5},{5... | collective-permute-start | bytes 995336 | tf_op jit(solution)/shard_map/ppermute | solution.py:17
  446.6 17.5 %collective-permute-start.6 = (f32[5184,16]{0,1:T(8,128)S(1)}, f32[5184,16]{0,1:T(8,128)}, u32[]{:S(2)}, u32[]{:S(2)}) collective-permute-start(f32[5184,16]{0,1:T(8,128)S(1)} %get-tuple-element.220), channel_id=1, source_target_pairs={{0,28},{4,0},{8,4},{12,8},{16,12},{20,16},{24,20},{28,24},{1,29},{... | collective-permute-start | bytes 995336 | tf_op jit(solution)/shard_map/ppermute | solution.py:17
  465.1 96.4 %collective-permute-start.5 = (f32[5184,16]{0,1:T(8,128)S(1)}, f32[5184,16]{0,1:T(8,128)S(1)}, u32[]{:S(2)}, u32[]{:S(2)}) collective-permute-start(f32[5184,16]{0,1:T(8,128)S(1)} %get-tuple-element.217), channel_id=1, source_target_pairs={{0,4},{4,8},{8,12},{12,16},{16,20},{20,24},{24,28},{28,0},{1,5},{5... | collective-permute-start | bytes 995336 | tf_op jit(solution)/shard_map/ppermute | solution.py:17
  465.4 96.1 %collective-permute-start.7 = (f32[5184,16]{0,1:T(8,128)S(1)}, f32[5184,16]{0,1:T(8,128)S(1)}, u32[]{:S(2)}, u32[]{:S(2)}) collective-permute-start(f32[5184,16]{0,1:T(8,128)S(1)} %get-tuple-element.218), channel_id=1, source_target_pairs={{0,28},{4,0},{8,4},{12,8},{16,12},{20,16},{24,20},{28,24},{1,29},{... | collective-permute-start | bytes 995336 | tf_op jit(solution)/shard_map/ppermute | solution.py:17
Sparse Core Ops, SparseCore 0:
  449.9 109.8 all-reduce.1
where the time goes:
time: 580 us; the launch traced here: 570 us
  matrix products  267 us (46%)
  local copies, waits for them, and re-layouts  147 us (25%)
  waiting for transfers between devices  103 us (18%)
  starting transfers between devices  17.7 us (3%)
  other arithmetic  15.6 us (3%)
  between operations  14.2 us (2%)
    dynamic_update_slice x64, local copies, waits for them, and re-layouts, local(): lax.scan(channel_step, jnp.zeros(radial_e.shape, jnp.float32), (gathered,...  89.9 us
    psum x1, waiting for transfers between devices, local(): lax.psum(jnp.transpose(weight_parts, (1, 0, 2)), ('atom', 'rep'))  86 us
    dot_general x64, matrix products, channel_terms(): jnp.dot(synth_table, filt_side, preferred_element_type=jnp.float32)  85.2 us
    dot_general x64, matrix products, channel_terms(): jnp.dot(synth_rows, grad_c, preferred_element_type=jnp.float32)  73.5 us
    dot_general x64, matrix products, channel_terms(): jnp.dot(synth_table, feat_side, preferred_element_type=jnp.float32)  70.1 us
    convert_element_type x64, local copies, waits for them, and re-layouts, basis_table(): return product.reshape(G, SAMPLES).astype(jnp.bfloat16)  22 us
    ppermute x8, starting transfers between devices, passed_along(): return lax.ppermute(value, axis, pairs)  17.6 us
    ppermute x8, waiting for transfers between devices, passed_along(): return lax.ppermute(value, axis, pairs)  17.2 us
  transfers between devices with their start and end apart: 9, of which 5 were waited for; matrix products, arithmetic and copies ran while one was open for 3% of the time, Pallas kernels for 0%

commit v1 on v0

v1 whole, which is shorter than its diff:
```python
import functools

import jax
import jax.numpy as jnp
import numpy as np
from jax import lax
from jax.experimental import pallas as pl
from jax.experimental.pallas import tpu as pltpu
from jax.sharding import PartitionSpec as P

BASIS = 9
POINTS = 13
SAMPLES = POINTS * POINTS
SAMPLES_PAD = -(-SAMPLES // 16) * 16
SLOTS = 32
REACH = 2
G = 81
G_PAD = 96
GROUP = 4


def basis_table():
    points = np.arange(POINTS) * (2.0 * np.pi / POINTS)
    degree_index = np.arange(BASIS)
    angles = ((degree_index + 1) // 2)[:, None] * points[None, :]
    single = np.where(
        degree_index[:, None] == 0,
        1.0,
        np.sqrt(2.0) * np.where(degree_index[:, None] % 2 == 1, np.cos(angles), np.sin(angles)),
    )
    product = (single[:, None, :, None] * single[None, :, None, :]).reshape(G, SAMPLES)
    padded = np.zeros((G_PAD, SAMPLES_PAD), np.float32)
    padded[:G, :SAMPLES] = product
    return padded


def passed_along(value, axis, steps):
    count = lax.axis_size(axis)
    pairs = [(source, (source + steps) % count) for source in range(count)]
    return lax.ppermute(value, axis, pairs)


def dot(a, b, contract=((1,), (0,))):
    return lax.dot_general(a, b, (contract, ((), ())), preferred_element_type=jnp.float32)


def edge_kernel(
    grad_ref, window_ref, wt_ref, sel_ref, rad_ref, table_ref, rows_ref, feat_ref, radial_ref, weight_ref
):
    bf16 = jnp.bfloat16

    @pl.when(pl.program_id(0) == 0)
    def _():
        radial_ref[...] = jnp.zeros_like(radial_ref)

    sel = sel_ref[...]
    rad = rad_ref[...]
    table = table_ref[...]
    rows = rows_ref[...]
    radial_sum = jnp.zeros(radial_ref.shape, jnp.float32)
    basis_count = radial_ref.shape[0]
    for c in range(GROUP):
        wt = wt_ref[c]
        gathered = dot(window_ref[c], sel, ((0,), (0,))).astype(bf16)
        weighted = dot(rows, grad_ref[c])
        filt_grid = dot(wt, rad, ((0,), (0,)))
        feat_side = (weighted * filt_grid).astype(bf16)
        edge_grad = dot(table, feat_side).astype(bf16)
        feat_grid = dot(rows, gathered)
        filt_side = (weighted * feat_grid).astype(bf16)
        both = dot(jnp.concatenate([table, wt], axis=0), filt_side)
        filt_grad = both[:G_PAD].astype(bf16)
        radial_sum = (
            radial_sum + both[G_PAD : G_PAD + basis_count] + both[G_PAD + basis_count :]
        )
        feat_ref[c] = (dot(sel, edge_grad, ((1,), (1,))) * (1.0 / SAMPLES))[:, :G]
        weight_ref[c] = dot(rad[:basis_count], filt_grad, ((1,), (1,)))[:, :G]
    radial_ref[...] += radial_sum


def edge_call(grad, window, wt, sel, rad, table, rows):
    chan_count, _, edges = grad.shape
    sources = sel.shape[0]
    basis_count = wt.shape[1] // 2
    whole = lambda x: pl.BlockSpec(x.shape, lambda i: (0,) * x.ndim)
    grouped = lambda shape: pl.BlockSpec((GROUP,) + shape, lambda i: (i, 0, 0))
    return pl.pallas_call(
        edge_kernel,
        grid=(chan_count // GROUP,),
        in_specs=[
            grouped((G, edges)),
            grouped((sources, G)),
            grouped(wt.shape[1:]),
            whole(sel),
            whole(rad),
            whole(table),
            whole(rows),
        ],
        out_specs=[
            grouped((sources, G)),
            pl.BlockSpec((basis_count, edges), lambda i: (0, 0)),
            grouped((basis_count, G)),
        ],
        out_shape=[
            jax.ShapeDtypeStruct((chan_count, sources, G), jnp.float32),
            jax.ShapeDtypeStruct((basis_count, edges), jnp.float32),
            jax.ShapeDtypeStruct((chan_count, basis_count, G), jnp.float32),
        ],
        compiler_params=pltpu.CompilerParams(vmem_limit_bytes=40 * 1024 * 1024),
        name="edges",
    )(grad, window, wt, sel, rad, table, rows)


def local(feats, neighbors, counts, radial, filter_weight, message_grad):
    exact = basis_table()
    table = jnp.asarray(exact, jnp.bfloat16)
    rows = jnp.asarray(exact[:G].T, jnp.bfloat16)
    atom_count = lax.axis_size("atom")
    position = lax.axis_index("atom")
    block_len = feats.shape[3]
    chan_count = feats.shape[1]
    own_block = jnp.transpose(feats[0], (0, 2, 1))
    window = jnp.concatenate(
        [
            own_block if offset == 0 else passed_along(own_block, "atom", -offset)
            for offset in range(-REACH, REACH + 1)
        ],
        axis=1,
    )
    window_len = window.shape[1]
    sources = neighbors[0].reshape(-1)
    slot_index = (
        sources // block_len - position + REACH
    ) % atom_count * block_len + sources % block_len
    valid = (jnp.arange(SLOTS, dtype=jnp.int32)[None, :] < counts[0][:, None]).reshape(-1)
    selector = (
        (slot_index[None, :] == jnp.arange(window_len, dtype=jnp.int32)[:, None]) & valid[None, :]
    ).astype(jnp.bfloat16)
    radial_e = radial[0] * valid.astype(jnp.bfloat16)[None, :]
    radial_twice = jnp.concatenate([radial_e, radial_e], axis=0)
    weight_grid = jnp.einsum(
        "kcg,gp->ckp",
        filter_weight,
        table[:G],
        preferred_element_type=jnp.float32,
    )
    coarse = lax.reduce_precision(weight_grid, 8, 7)
    weight_parts = jnp.concatenate([coarse, weight_grid - coarse], axis=1).astype(jnp.bfloat16)
    window_grad, radial_local, weight_local = edge_call(
        message_grad[0], window, weight_parts, selector, radial_twice, table, rows
    )

    def block_of(offset):
        return window_grad[:, (offset + REACH) * block_len : (offset + REACH + 1) * block_len]

    returned_sum = block_of(0)
    for direction in (1, -1):
        carried = block_of(direction * REACH)
        for offset in range(REACH - 1, -1, -1):
            arrived = passed_along(carried, "atom", direction)
            if offset > 0:
                carried = arrived + block_of(direction * offset)
            else:
                returned_sum = returned_sum + arrived
    feat_grad = jnp.transpose(returned_sum, (0, 2, 1))[None]
    radial_grad = lax.psum(radial_local, "chan")[None] * (1.0 / SAMPLES)
    weight_summed = lax.psum(jnp.transpose(weight_local, (1, 0, 2)), ("atom", "rep"))
    weight_grad = weight_summed / (SAMPLES * atom_count * block_len * lax.axis_size("rep"))
    return (feat_grad, radial_grad, weight_grad)


def solution(mesh):
    placed = (
        P("rep", "chan", None, "atom"),
        P("rep", "atom", None),
        P("rep", "atom"),
        P("rep", None, "atom"),
        P(None, "chan", None),
        P("rep", "chan", None, "atom"),
    )
    return jax.shard_map(
        local,
        mesh=mesh,
        in_specs=placed,
        out_specs=(P("rep", "chan", None, "atom"), P("rep", None, "atom"), P(None, "chan", None)),
        check_vma=False,
    )
```

time: 580 us -> 212 us (0.37); the launches traced: 570 us -> 211 us
  matrix products: 267 us -> 0.99 us
  local copies, waits for them, and re-layouts: 147 us -> 8.41 us
  Pallas kernels: 0 us -> 42.4 us
  waiting for transfers between devices: 103 us -> 118 us
  other arithmetic: 15.6 us -> 6.87 us
    dot_general x386 -> x1, matrix products: 267 us -> 0.99 us  [local(): jnp.einsum('kcg,gp->ckp', filter_weight, table[:G], preferred_element_typ...]
    dynamic_update_slice x64 -> x0, local copies, waits for them, and re-layouts: 89.9 us -> none  [local(): lax.scan(channel_step, jnp.zeros(radial_e.shape, jnp.float32), (gathered,...]
    pallas_call x0 -> x1, Pallas kernels: none -> 42.4 us  [edge_call(): pl.pallas_call(edge_kernel, grid=(chan_count // GROUP,), in_specs=[groupe...]
    convert_element_type x128 -> x0, local copies, waits for them, and re-layouts: 27.1 us -> none  [the longest x64 22 us: basis_table(): return product.reshape(G, SAMPLES).astype(jnp.bfloat16)]
    reshape x3 -> x0, local copies, waits for them, and re-layouts: 16.6 us -> none  [the longest x1 7.91 us: local(): gathered = gathered.astype(jnp.bfloat16).reshape(chan_count, G, -1)]
    convert_element_type x129 -> x2, other arithmetic: 12.2 us -> 0.04 us  [the longest x1 0.03 us: local(): selector = ((slot_index[None, :] == jnp.arange(window_len, dtype=jnp.int3...]
    psum x1, waiting for transfers between devices: 86 us -> 93.3 us  [local(): lax.psum(jnp.transpose(weight_local, (1, 0, 2)), ('atom', 'rep'))]
    ppermute x8, waiting for transfers between devices: 17.2 us -> 24.4 us  [passed_along(): return lax.ppermute(value, axis, pairs)]
  transfers between devices with their start and end apart: 9 -> 9, of which waited for: 5 -> 4; matrix products, arithmetic and copies ran while one was open for 3% -> 6% of each run, Pallas kernels for 0% -> 0%
where the time goes in v1:
time: 212 us; the launch traced here: 211 us
  waiting for transfers between devices  118 us (56%)
  Pallas kernels  42.4 us (20%)
  starting transfers between devices  17.5 us (8%)
  between operations  14.2 us (7%)
  local copies, waits for them, and re-layouts  8.41 us (4%)
  other arithmetic  6.87 us (3%)
  blocking collectives  3.36 us (2%)
    psum x1, waiting for transfers between devices, local(): lax.psum(jnp.transpose(weight_local, (1, 0, 2)), ('atom', 'rep'))  93.3 us
    pallas_call x1, Pallas kernels, edge_call(): pl.pallas_call(edge_kernel, grid=(chan_count // GROUP,), in_specs=[groupe...  42.4 us
    ppermute x8, waiting for transfers between devices, passed_along(): return lax.ppermute(value, axis, pairs)  24.4 us
    ppermute x8, starting transfers between devices, passed_along(): return lax.ppermute(value, axis, pairs)  17.5 us
    unnamed x16, local copies, waits for them, and re-layouts  6.47 us
  transfers between devices with their start and end apart: 9, of which 4 were waited for; matrix products, arithmetic and copies ran while one was open for 6% of the time, Pallas kernels for 0%

profile of v1, /device:TPU:0, one launch (start us, length us, event | category | flops | bytes accessed | tf_op | source)
XLA Modules:
  0.0 211.5 jit_solution(17988151237331622046)
XLA Ops:
  7.2 5.1 %collective-permute-start.3 = (bf16[64,16,81]{2,1,0:T(8,128)(2,1)}, bf16[64,16,81]{2,1,0:T(8,128)(2,1)S(1)}, u32[]{:S(2)}, u32[]{:S(2)}) collective-permute-start(bf16[64,16,81]{2,1,0:T(8,128)(2,1)} %bitcast.24), channel_id=1, source_target_pairs={{0,24},{4,28},{8,0},{12,4},{16,8},{20,12},{24,16},{28,20},{1,25},{... | collective-permute-start | bytes 497672 | tf_op jit(solution)/shard_map/ppermute | solution.py:40
  12.3 1.4 collective-permute-start.2
  13.7 0.6 collective-permute-start.1
  14.4 0.9 collective-permute-start
  15.3 0.8 reshape_squeeze.3
  16.1 0.7 iota_compare_fusion.1
  17.0 1.0 fusion.10
  18.0 0.3 reduce-precision_convert_fusion
  18.4 5.6 %copy.17 = bf16[1,64,81,512]{3,2,1,0:T(8,128)(2,1)S(1)} copy(bf16[1,64,81,512]{3,1,2,0:T(8,128)(2,1)} %param.13) | data formatting | bytes 10616832 | tf_op args[5]
  24.0 6.3 %collective-permute-done = bf16[64,16,81]{2,1,0:T(8,128)(2,1)S(1)} collective-permute-done((bf16[64,16,81]{2,1,0:T(8,128)(2,1)}, bf16[64,16,81]{2,1,0:T(8,128)(2,1)S(1)}, u32[]{:S(2)}, u32[]{:S(2)}) %collective-permute-start) | collective-permute-done | bytes 165920 | tf_op jit(solution)/shard_map/ppermute | solution.py:40
  30.6 42.4 %edges.1 = (f32[64,80,81]{2,1,0:T(8,128)S(1)}, f32[8,512]{1,0:T(8,128)S(1)}, f32[64,8,81]{2,1,0:T(8,128)}) custom-call(bf16[64,81,512]{2,1,0:T(8,128)(2,1)S(1)} %bitcast.23, bf16[64,80,81]{2,1,0:T(8,128)(2,1)S(1)} %constant_dynamic-update-slice_fusion.window_ref, bf16[64,16,176]{2,1,0:T(8,128)(2,1)S(1)} %pad_maximum_fusion.wt_ref, ...), custom_call_target="tpu_custom_call" | custom-call | tf_op jit(solution)/shard_map/edges/pallas_call | solution.py:87
  73.0 1.0 fusion.9
  74.0 1.4 collective-permute-start.4
  75.5 3.3 %collective-permute-start.6 = (f32[64,16,81]{2,1,0:T(8,128)}, f32[64,16,81]{2,1,0:T(8,128)}, u32[]{:S(2)}, u32[]{:S(2)}) collective-permute-start(f32[64,16,81]{2,1,0:T(8,128)} %get-tuple-element.15), channel_id=1, source_target_pairs={{0,28},{4,0},{8,4},{12,8},{16,12},{20,16},{24,20},{28,24},{1,29},{... | collective-permute-start | bytes 995336 | tf_op jit(solution)/shard_map/ppermute | solution.py:40
  78.8 3.4 %psum.14 = f32[8,512]{1,0:T(8,128)S(1)} all-reduce(f32[8,512]{1,0:T(8,128)S(1)} %get-tuple-element.7), channel_id=1, replica_groups=mesh['atom'=8,'chan'=2,'rep'=2] {'chan'}, use_global_device_ids=true, to_apply=%region_0.1 | all-reduce | flops 4096 | bytes 32768 | tf_op jit(solution)/shard_map/psum | solution.py:166
  82.1 15.9 %collective-permute-done.4 = f32[64,16,81]{2,1,0:T(8,128)S(1)} collective-permute-done((f32[64,16,81]{2,1,0:T(8,128)}, f32[64,16,81]{2,1,0:T(8,128)S(1)}, u32[]{:S(2)}, u32[]{:S(2)}) %collective-permute-start.4) | collective-permute-done | bytes 331808 | tf_op jit(solution)/shard_map/ppermute | solution.py:40
  98.0 2.2 %collective-permute-done.6 = f32[64,16,81]{2,1,0:T(8,128)} collective-permute-done((f32[64,16,81]{2,1,0:T(8,128)}, f32[64,16,81]{2,1,0:T(8,128)}, u32[]{:S(2)}, u32[]{:S(2)}) %collective-permute-start.6) | collective-permute-done | bytes 331808 | tf_op jit(solution)/shard_map/ppermute | solution.py:40
  100.2 2.1 %slice_add_fusion.1 = (f32[64,16,81]{2,1,0:T(8,128)}, f32[64,16,81]{2,1,0:T(8,128)}) fusion(f32[64,16,81]{2,1,0:T(8,128)S(1)} %collective-permute-done.4, f32[64,80,81]{2,1,0:T(8,128)S(1)} %get-tuple-element.6, f32[64,16,81]{2,1,0:T(8,128)} %collective-permute-done.6), kind=kLoop, calls=%fused_computation.7 | loop fusion | flops 165888 | bytes 1990656 | tf_op jit(solution)/shard_map/add | solution.py:162
  102.6 4.5 %collective-permute-start.7 = (f32[64,16,81]{2,1,0:T(8,128)}, f32[64,16,81]{2,1,0:T(8,128)}, u32[]{:S(2)}, u32[]{:S(2)}) collective-permute-start(f32[64,16,81]{2,1,0:T(8,128)} %get-tuple-element.13), channel_id=1, source_target_pairs={{0,28},{4,0},{8,4},{12,8},{16,12},{20,16},{24,20},{28,24},{1,29},{... | collective-permute-start | bytes 995336 | tf_op jit(solution)/shard_map/ppermute | solution.py:40
  107.1 0.6 multiply_bitcast_fusion
  107.7 93.3 %all-reduce.2.cloned.1.call-done = f32[8,64,81]{2,0,1:T(8,128)} async-done(((f32[8,64,81]{2,0,1:T(8,128)}), f32[8,64,81]{2,0,1:T(8,128)}) %all-reduce.2.cloned.1.call-update) | async-done | bytes 165904 | tf_op jit(solution)/shard_map/psum | solution.py:167
  201.0 1.0 broadcast_multiply_fusion
  201.9 0.8 copy.13
  202.7 1.9 add_bitcast_fusion
  (30 shorter events, 0.7 us)
Async XLA Ops:
  7.2 9.8 %copy-start = (bf16[8,64,81]{2,1,0:T(8,128)(2,1)S(1)}, bf16[8,64,81]{2,1,0:T(8,128)(2,1)}, u32[]{:S(2)}) copy-start(bf16[8,64,81]{2,1,0:T(8,128)(2,1)} %param.12) | copy-start | bytes 248836
  7.2 11.1 %copy-start.4 = (bf16[1,8,512]{2,1,0:T(8,128)(2,1)S(1)}, bf16[1,8,512]{2,1,0:T(8,128)(2,1)}, u32[]{:S(2)}) copy-start(bf16[1,8,512]{2,1,0:T(8,128)(2,1)} %param.11) | copy-start | bytes 24580
  7.2 193.8 %all-reduce.2.cloned.1.call-start = ((), (), s32[]{:S(2)}) async-start(), calls=%async_computation | async-start | bytes 524288 | tf_op jit(solution)/shard_map/psum | solution.py:167
  7.2 23.3 %collective-permute-start.3 = (bf16[64,16,81]{2,1,0:T(8,128)(2,1)}, bf16[64,16,81]{2,1,0:T(8,128)(2,1)S(1)}, u32[]{:S(2)}, u32[]{:S(2)}) collective-permute-start(bf16[64,16,81]{2,1,0:T(8,128)(2,1)} %bitcast.24), channel_id=1, source_target_pairs={{0,24},{4,28},{8,0},{12,4},{16,8},{20,12},{24,16},{28,20},{1,25},{... | collective-permute-start | bytes 497672 | tf_op jit(solution)/shard_map/ppermute | solution.py:40
  12.3 18.1 %collective-permute-start.2 = (bf16[64,16,81]{2,1,0:T(8,128)(2,1)}, bf16[64,16,81]{2,1,0:T(8,128)(2,1)S(1)}, u32[]{:S(2)}, u32[]{:S(2)}) collective-permute-start(bf16[64,16,81]{2,1,0:T(8,128)(2,1)} %bitcast.25), channel_id=1, source_target_pairs={{0,28},{4,0},{8,4},{12,8},{16,12},{20,16},{24,20},{28,24},{1,29},{... | collective-permute-start | bytes 497672 | tf_op jit(solution)/shard_map/ppermute | solution.py:40
  13.7 16.6 %collective-permute-start.1 = (bf16[64,16,81]{2,1,0:T(8,128)(2,1)}, bf16[64,16,81]{2,1,0:T(8,128)(2,1)S(1)}, u32[]{:S(2)}, u32[]{:S(2)}) collective-permute-start(bf16[64,16,81]{2,1,0:T(8,128)(2,1)} %bitcast.26), channel_id=1, source_target_pairs={{0,4},{4,8},{8,12},{12,16},{16,20},{20,24},{24,28},{28,0},{1,5},{5... | collective-permute-start | bytes 497672 | tf_op jit(solution)/shard_map/ppermute | solution.py:40
  14.4 15.9 %collective-permute-start = (bf16[64,16,81]{2,1,0:T(8,128)(2,1)}, bf16[64,16,81]{2,1,0:T(8,128)(2,1)S(1)}, u32[]{:S(2)}, u32[]{:S(2)}) collective-permute-start(bf16[64,16,81]{2,1,0:T(8,128)(2,1)} %bitcast.27), channel_id=1, source_target_pairs={{0,8},{4,12},{8,16},{12,20},{16,24},{20,28},{24,0},{28,4},{1,9},{5... | collective-permute-start | bytes 497672 | tf_op jit(solution)/shard_map/ppermute | solution.py:40
  18.4 12.0 %copy-start.3 = (bf16[1,64,81,16]{2,3,1,0:T(8,128)(2,1)S(1)}, bf16[1,64,81,16]{2,3,1,0:T(8,128)(2,1)}, u32[]{:S(2)}) copy-start(bf16[1,64,81,16]{2,3,1,0:T(8,128)(2,1)} %param.8) | copy-start | bytes 497668
  24.0 6.6 %copy-start.1 = (bf16[96,176]{1,0:T(8,128)(2,1)S(1)}, bf16[96,176]{1,0:T(8,128)(2,1)}, u32[]{:S(2)}) copy-start(bf16[96,176]{1,0:T(8,128)(2,1)} %constant.57.clone.table_ref) | copy-start | bytes 101380
  24.0 6.6 %copy-start.2 = (bf16[176,81]{1,0:T(8,128)(2,1)S(1)}, bf16[176,81]{1,0:T(8,128)(2,1)}, u32[]{:S(2)}) copy-start(bf16[176,81]{1,0:T(8,128)(2,1)} %constant.58.clone.rows_ref) | copy-start | bytes 85540
  74.0 24.0 %collective-permute-start.4 = (f32[64,16,81]{2,1,0:T(8,128)}, f32[64,16,81]{2,1,0:T(8,128)S(1)}, u32[]{:S(2)}, u32[]{:S(2)}) collective-permute-start(f32[64,16,81]{2,1,0:T(8,128)} %get-tuple-element.14), channel_id=1, source_target_pairs={{0,4},{4,8},{8,12},{12,16},{16,20},{20,24},{24,28},{28,0},{1,5},{5... | collective-permute-start | bytes 995336 | tf_op jit(solution)/shard_map/ppermute | solution.py:40
  75.5 24.8 %collective-permute-start.6 = (f32[64,16,81]{2,1,0:T(8,128)}, f32[64,16,81]{2,1,0:T(8,128)}, u32[]{:S(2)}, u32[]{:S(2)}) collective-permute-start(f32[64,16,81]{2,1,0:T(8,128)} %get-tuple-element.15), channel_id=1, source_target_pairs={{0,28},{4,0},{8,4},{12,8},{16,12},{20,16},{24,20},{28,24},{1,29},{... | collective-permute-start | bytes 995336 | tf_op jit(solution)/shard_map/ppermute | solution.py:40
  102.4 100.3 %collective-permute-start.5 = (f32[64,16,81]{2,1,0:T(8,128)}, f32[64,16,81]{2,1,0:T(8,128)S(1)}, u32[]{:S(2)}, u32[]{:S(2)}) collective-permute-start(f32[64,16,81]{2,1,0:T(8,128)} %get-tuple-element.12), channel_id=1, source_target_pairs={{0,4},{4,8},{8,12},{12,16},{16,20},{20,24},{24,28},{28,0},{1,5},{5... | collective-permute-start | bytes 995336 | tf_op jit(solution)/shard_map/ppermute | solution.py:40
  102.6 100.1 %collective-permute-start.7 = (f32[64,16,81]{2,1,0:T(8,128)}, f32[64,16,81]{2,1,0:T(8,128)}, u32[]{:S(2)}, u32[]{:S(2)}) collective-permute-start(f32[64,16,81]{2,1,0:T(8,128)} %get-tuple-element.13), channel_id=1, source_target_pairs={{0,28},{4,0},{8,4},{12,8},{16,12},{20,16},{24,20},{28,24},{1,29},{... | collective-permute-start | bytes 995336 | tf_op jit(solution)/shard_map/ppermute | solution.py:40
Sparse Core Ops, SparseCore 0:
  78.9 122.0 all-reduce.1

commit v2 on v1

v2 whole, which is shorter than its diff:
```python
import functools

import jax
import jax.numpy as jnp
import numpy as np
from jax import lax
from jax.experimental import pallas as pl
from jax.experimental.pallas import tpu as pltpu
from jax.sharding import PartitionSpec as P

BASIS = 9
POINTS = 13
SAMPLES = POINTS * POINTS
SAMPLES_PAD = -(-SAMPLES // 16) * 16
SLOTS = 32
REACH = 2
G = 81
G_PAD = 96
GROUP = 4


def basis_table():
    points = np.arange(POINTS) * (2.0 * np.pi / POINTS)
    degree_index = np.arange(BASIS)
    angles = ((degree_index + 1) // 2)[:, None] * points[None, :]
    single = np.where(
        degree_index[:, None] == 0,
        1.0,
        np.sqrt(2.0) * np.where(degree_index[:, None] % 2 == 1, np.cos(angles), np.sin(angles)),
    )
    product = (single[:, None, :, None] * single[None, :, None, :]).reshape(G, SAMPLES)
    padded = np.zeros((G_PAD, SAMPLES_PAD), np.float32)
    padded[:G, :SAMPLES] = product
    return padded


def passed_along(value, axis, steps):
    count = lax.axis_size(axis)
    pairs = [(source, (source + steps) % count) for source in range(count)]
    return lax.ppermute(value, axis, pairs)


def dot(a, b, contract=((1,), (0,))):
    return lax.dot_general(a, b, (contract, ((), ())), preferred_element_type=jnp.float32)


def feature_kernel(
    grad_ref, wt_ref, sel_ref, rad_ref, table_ref, rows_ref, grid_ref, own_ref, *sent_refs
):
    bf16 = jnp.bfloat16
    sel = sel_ref[...]
    rad = rad_ref[...]
    table = table_ref[...]
    rows = rows_ref[...]
    block_len = own_ref.shape[1]
    for c in range(GROUP):
        weighted = dot(rows, grad_ref[c])
        filt_grid = dot(wt_ref[c], rad)
        grid_ref[c] = weighted.astype(bf16)
        feat_side = (weighted * filt_grid).astype(bf16)
        edge_grad = dot(table, feat_side).astype(bf16)
        placed = (dot(sel, edge_grad, ((1,), (1,))) * (1.0 / SAMPLES))[:, :G]
        blocks = [
            placed[index * block_len : (index + 1) * block_len] for index in range(2 * REACH + 1)
        ]
        own_ref[c] = blocks.pop(REACH)
        for sent_ref, block in zip(sent_refs, blocks):
            sent_ref[c] = block.astype(bf16)


def filter_kernel(
    grid_ref, wt_ref, sel_ref, rad_ref, table_ref, rows_ref, *refs
):
    bf16 = jnp.bfloat16
    window_refs, (radial_ref, weight_ref) = refs[:-2], refs[-2:]

    @pl.when(pl.program_id(0) == 0)
    def _():
        radial_ref[...] = jnp.zeros_like(radial_ref)

    sel = sel_ref[...]
    table = table_ref[...]
    rows = rows_ref[...]
    basis_count = radial_ref.shape[0]
    rad = rad_ref[:basis_count]
    radial_sum = jnp.zeros(radial_ref.shape, jnp.float32)
    for c in range(GROUP):
        window = jnp.concatenate([ref[c] for ref in window_refs], axis=0)
        atom_grid = dot(rows, window, ((1,), (1,))).astype(bf16)
        feat_grid = dot(atom_grid, sel)
        filt_side = (grid_ref[c].astype(jnp.float32) * feat_grid).astype(bf16)
        both = dot(jnp.concatenate([table, wt_ref[c]], axis=0), filt_side)
        filt_grad = both[:G_PAD].astype(bf16)
        radial_sum = (
            radial_sum + both[G_PAD : G_PAD + basis_count] + both[G_PAD + basis_count :]
        )
        weight_ref[c] = dot(rad, filt_grad, ((1,), (1,)))[:, :G]
    radial_ref[...] += radial_sum


def whole(x):
    return pl.BlockSpec(x.shape, lambda i: (0,) * x.ndim)


def grouped(shape):
    return pl.BlockSpec((GROUP,) + tuple(shape), lambda i: (i, 0, 0))


def grid_call(kernel, name, out_shape, out_specs, split, shared, split_last=()):
    chan_count = split[0].shape[0]
    return pl.pallas_call(
        kernel,
        grid=(chan_count // GROUP,),
        in_specs=[grouped(x.shape[1:]) for x in split]
        + [whole(x) for x in shared]
        + [grouped(x.shape[1:]) for x in split_last],
        out_specs=out_specs,
        out_shape=out_shape,
        compiler_params=pltpu.CompilerParams(vmem_limit_bytes=54 * 1024 * 1024),
        cost_estimate=pl.CostEstimate(
            flops=chan_count * 160_000_000, bytes_accessed=16_000_000, transcendentals=0
        ),
        name=name,
    )(*split, *shared, *split_last)


def sum_kernel(
    weight_ref, radial_ref, weight_out, radial_out, parts, slots, send1, recv1, send2, recv2, send3, recv3
):
    atoms, reps, chans = (lax.axis_size(name) for name in ("atom", "rep", "chan"))
    atom, rep, chan = (lax.axis_index(name) for name in ("atom", "rep", "chan"))
    count = atoms * reps
    me = atom * reps + rep

    def member(step):
        index = lax.rem(me + step, count)
        return index, {"atom": index // reps, "chan": chan, "rep": lax.rem(index, reps)}

    def other(step):
        return {"atom": atom, "chan": lax.rem(chan + step, chans), "rep": rep}

    barrier = pltpu.get_barrier_semaphore()

    @pl.loop(1, count)
    def _(step):
        pl.semaphore_signal(
            barrier, inc=1, device_id=member(step)[1], device_id_type=pl.DeviceIdType.MESH
        )

    for step in range(1, chans):
        pl.semaphore_signal(
            barrier, inc=1, device_id=other(step), device_id_type=pl.DeviceIdType.MESH
        )
    pl.semaphore_wait(barrier, count - 1 + chans - 1)

    def chunk_copy(step):
        index, device = member(step)
        return pltpu.make_async_remote_copy(
            src_ref=weight_ref.at[index],
            dst_ref=parts.at[step],
            send_sem=send1.at[step],
            recv_sem=recv1.at[step],
            device_id=device,
            device_id_type=pl.DeviceIdType.MESH,
        )

    def radial_copy(step):
        return pltpu.make_async_remote_copy(
            src_ref=radial_ref,
            dst_ref=slots.at[chan],
            send_sem=send2.at[step],
            recv_sem=recv2.at[step],
            device_id=other(step),
            device_id_type=pl.DeviceIdType.MESH,
        )

    def total_copy(step):
        return pltpu.make_async_remote_copy(
            src_ref=weight_out.at[me],
            dst_ref=weight_out.at[me],
            send_sem=send3.at[step],
            recv_sem=recv3.at[step],
            device_id=member(step)[1],
            device_id_type=pl.DeviceIdType.MESH,
        )

    @pl.loop(1, count)
    def _(step):
        chunk_copy(step).start()

    for step in range(1, chans):
        radial_copy(step).start()
    slots[chan] = radial_ref[...]

    @pl.loop(1, count)
    def _(step):
        chunk_copy(step).wait_recv()

    total = weight_ref[me]
    for step in range(1, count):
        total = total + parts[step]
    weight_out[me] = total

    @pl.loop(1, count)
    def _(step):
        total_copy(step).start()

    for step in range(1, chans):
        radial_copy(step).wait()
    radial_total = slots[0]
    for index in range(1, chans):
        radial_total = radial_total + slots[index]
    radial_out[...] = radial_total * (1.0 / SAMPLES)

    @pl.loop(1, count)
    def _(step):
        chunk_copy(step).wait_send()
        total_copy(step).wait()


def sum_call(weight, radial):
    chans = lax.axis_size("chan")
    count = weight.shape[0]
    vmem = pl.BlockSpec(memory_space=pltpu.VMEM)
    sems = [pltpu.SemaphoreType.DMA((size,)) for size in (count, count, chans, chans, count, count)]
    return pl.pallas_call(
        sum_kernel,
        in_specs=[vmem, vmem],
        out_specs=[vmem, vmem],
        out_shape=[
            jax.ShapeDtypeStruct(weight.shape, jnp.float32),
            jax.ShapeDtypeStruct(radial.shape, jnp.float32),
        ],
        scratch_shapes=[
            pltpu.VMEM(weight.shape, jnp.float32),
            pltpu.VMEM((chans,) + radial.shape, jnp.float32),
        ]
        + sems,
        compiler_params=pltpu.CompilerParams(
            collective_id=0, has_side_effects=True, vmem_limit_bytes=16 * 1024 * 1024
        ),
        name="sums",
    )(weight, radial)


def local(feats, neighbors, counts, radial, filter_weight, message_grad):
    exact = basis_table()
    table = jnp.asarray(exact, jnp.bfloat16)
    rows = jnp.asarray(exact[:G].T, jnp.bfloat16)
    atom_count = lax.axis_size("atom")
    position = lax.axis_index("atom")
    block_len = feats.shape[3]
    chan_count = feats.shape[1]
    own_block = jnp.transpose(feats[0], (0, 2, 1))
    offsets = [offset for offset in range(-REACH, REACH + 1)]
    window = [
        own_block if offset == 0 else passed_along(own_block, "atom", -offset)
        for offset in offsets
    ]
    window_len = len(offsets) * block_len
    sources = neighbors[0].reshape(-1)
    slot_index = (
        sources // block_len - position + REACH
    ) % atom_count * block_len + sources % block_len
    valid = (jnp.arange(SLOTS, dtype=jnp.int32)[None, :] < counts[0][:, None]).reshape(-1)
    selector = (
        (slot_index[None, :] == jnp.arange(window_len, dtype=jnp.int32)[:, None]) & valid[None, :]
    ).astype(jnp.bfloat16)
    radial_e = radial[0] * valid.astype(jnp.bfloat16)[None, :]
    radial_twice = jnp.concatenate([radial_e, radial_e], axis=0)
    weight_grid = jnp.einsum(
        "kcg,gp->ckp", filter_weight, table[:G], preferred_element_type=jnp.float32
    )
    coarse = lax.reduce_precision(weight_grid, 8, 7)
    weight_parts = jnp.concatenate([coarse, weight_grid - coarse], axis=1).astype(jnp.bfloat16)
    basis_count = radial_e.shape[0]
    edges = radial_e.shape[1]
    block_shape = (chan_count, block_len, G)
    grid, own_grad, *outgoing = grid_call(
        feature_kernel,
        "feature_path",
        [
            jax.ShapeDtypeStruct((chan_count, SAMPLES_PAD, edges), jnp.bfloat16),
            jax.ShapeDtypeStruct(block_shape, jnp.float32),
        ]
        + [jax.ShapeDtypeStruct(block_shape, jnp.bfloat16)] * (2 * REACH),
        [grouped((SAMPLES_PAD, edges))] + [grouped(block_shape[1:])] * (2 * REACH + 1),
        [message_grad[0], jnp.transpose(weight_parts, (0, 2, 1))],
        [selector, radial_twice, table, rows],
    )
    arrived = [
        passed_along(block, "atom", offset)
        for offset, block in zip([o for o in offsets if o != 0], outgoing)
    ]
    radial_local, weight_local = grid_call(
        filter_kernel,
        "filter_path",
        [
            jax.ShapeDtypeStruct((basis_count, edges), jnp.float32),
            jax.ShapeDtypeStruct((chan_count, basis_count, G), jnp.float32),
        ],
        [
            pl.BlockSpec((basis_count, edges), lambda i: (0, 0)),
            grouped((basis_count, G)),
        ],
        [grid, weight_parts],
        [selector, radial_twice, table, rows],
        window,
    )
    sharers = atom_count * lax.axis_size("rep")
    weight_summed, radial_grad = sum_call(weight_local.reshape(sharers, -1, G), radial_local)
    weight_summed = jnp.transpose(weight_summed.reshape(chan_count, basis_count, G), (1, 0, 2))
    weight_grad = weight_summed * (1.0 / (SAMPLES * sharers * block_len))
    returned_sum = own_grad
    for block in arrived:
        returned_sum = returned_sum + block.astype(jnp.float32)
    feat_grad = jnp.transpose(returned_sum, (0, 2, 1))[None]
    return (feat_grad, radial_grad[None], weight_grad)


def solution(mesh):
    placed = (
        P("rep", "chan", None, "atom"),
        P("rep", "atom", None),
        P("rep", "atom"),
        P("rep", None, "atom"),
        P(None, "chan", None),
        P("rep", "chan", None, "atom"),
    )
    return jax.shard_map(
        local,
        mesh=mesh,
        in_specs=placed,
        out_specs=(P("rep", "chan", None, "atom"), P("rep", None, "atom"), P(None, "chan", None)),
        check_vma=False,
    )
```

time: 212 us -> 110 us (0.52)
  waiting for transfers between devices: 118 us -> 0.02 us
  Pallas kernels: 42.4 us -> 77.4 us
  between operations: 14.2 us -> 0.74 us
  local copies, waits for them, and re-layouts: 8.41 us -> 14.6 us
  starting transfers between devices: 17.5 us -> 12.2 us
  blocking collectives: 3.36 us -> 0 us
  other arithmetic: 6.87 us -> 3.54 us
    psum x1 -> x0, waiting for transfers between devices: 93.3 us -> none  [local(): lax.psum(jnp.transpose(weight_local, (1, 0, 2)), ('atom', 'rep'))]
    pallas_call x1 -> x3, Pallas kernels: 42.4 us -> 77.4 us  [the longest x2 58.7 us: grid_call(): pl.pallas_call(kernel, grid=(chan_count // GROUP,), in_specs=[grouped(x.s...]
    ppermute x8, waiting for transfers between devices: 24.4 us -> 0.02 us  [passed_along(): return lax.ppermute(value, axis, pairs)]
    ppermute x8, starting transfers between devices: 17.5 us -> 12.2 us  [passed_along(): return lax.ppermute(value, axis, pairs)]
    unnamed x16 -> x24, local copies, waits for them, and re-layouts: 6.47 us -> 11 us
    psum x1 -> x0, blocking collectives: 3.36 us -> none  [local(): radial_grad = lax.psum(radial_local, 'chan')[None] * (1.0 / SAMPLES)]
    transpose x0 -> x1, local copies, waits for them, and re-layouts: none -> 2.67 us  [local(): jnp.transpose(weight_parts, (0, 2, 1))]
    add x1 -> x0, other arithmetic: 2.15 us -> none  [local(): carried = arrived + block_of(direction * offset)]
  transfers between devices with their start and end apart: 9 -> 8, of which waited for: 4 -> 0; matrix products, arithmetic and copies ran while one was open for 6% -> 14% of each run, Pallas kernels for 0% -> 71%
where the time goes in v2:
time: 110 us
  Pallas kernels  77.4 us (70%)
  local copies, waits for them, and re-layouts  14.6 us (13%)
  starting transfers between devices  12.2 us (11%)
  other arithmetic  3.54 us (3%)
    pallas_call x2, Pallas kernels, grid_call(): pl.pallas_call(kernel, grid=(chan_count // GROUP,), in_specs=[grouped(x.s...  58.7 us
    pallas_call x1, Pallas kernels, sum_call(): pl.pallas_call(sum_kernel, in_specs=[vmem, vmem], out_specs=[vmem, vmem],...  18.7 us
    ppermute x8, starting transfers between devices, passed_along(): return lax.ppermute(value, axis, pairs)  12.2 us
    unnamed x24, local copies, waits for them, and re-layouts  11 us
    transpose x1, local copies, waits for them, and re-layouts, local(): jnp.transpose(weight_parts, (0, 2, 1))  2.67 us
  transfers between devices with their start and end apart: 8, of which 0 were waited for; matrix products, arithmetic and copies ran while one was open for 14% of the time, Pallas kernels for 71%

profile of v2, /device:TPU:0, one launch (start us, length us, event | category | flops | bytes accessed | tf_op | source)
XLA Modules:
  0.0 109.5 jit_solution(15826124650544207748)
XLA Ops:
  0.7 3.1 %collective-permute-start.4 = (bf16[64,16,81]{2,1,0:T(8,128)(2,1)}, bf16[64,16,81]{2,1,0:T(8,128)(2,1)S(1)}, u32[]{:S(2)}, u32[]{:S(2)}) collective-permute-start(bf16[64,16,81]{2,1,0:T(8,128)(2,1)} %bitcast.33), channel_id=1, source_target_pairs={{0,8},{4,12},{8,16},{12,20},{16,24},{20,28},{24,0},{28,4},{1,9},{5... | collective-permute-start | bytes 497672 | tf_op jit(solution)/shard_map/ppermute | solution.py:40
  3.8 1.5 %collective-permute-start.5 = (bf16[64,16,81]{2,1,0:T(8,128)(2,1)}, bf16[64,16,81]{2,1,0:T(8,128)(2,1)S(1)}, u32[]{:S(2)}, u32[]{:S(2)}) collective-permute-start(bf16[64,16,81]{2,1,0:T(8,128)(2,1)} %bitcast.34), channel_id=1, source_target_pairs={{0,4},{4,8},{8,12},{12,16},{16,20},{20,24},{24,28},{28,0},{1,5},{5... | collective-permute-start | bytes 497672 | tf_op jit(solution)/shard_map/ppermute | solution.py:40
  5.2 3.2 %collective-permute-start.6 = (bf16[64,16,81]{2,1,0:T(8,128)(2,1)}, bf16[64,16,81]{2,1,0:T(8,128)(2,1)S(1)}, u32[]{:S(2)}, u32[]{:S(2)}) collective-permute-start(bf16[64,16,81]{2,1,0:T(8,128)(2,1)} %bitcast.35), channel_id=1, source_target_pairs={{0,28},{4,0},{8,4},{12,8},{16,12},{20,16},{24,20},{28,24},{1,29},{... | collective-permute-start | bytes 497672 | tf_op jit(solution)/shard_map/ppermute | solution.py:40
  8.5 0.3 collective-permute-start.7
  8.8 1.0 fusion.10
  9.8 0.3 reduce-precision_convert_fusion
  10.1 0.9 pad_maximum_fusion
  11.0 2.7 %copy.13.wt_ref = bf16[64,176,16]{2,1,0:T(8,128)(2,1)} copy(bf16[64,176,16]{1,2,0:T(8,128)(2,1)S(1)} %get-tuple-element.24) | data formatting | bytes 720896 | tf_op jit(solution)/shard_map/transpose | solution.py:288
  13.9 0.7 fusion.2.sel_ref
  14.6 0.6 pad_maximum_fusion.1.rad_ref
  15.2 8.0 %copy.19 = bf16[1,64,81,512]{3,2,1,0:T(8,128)(2,1)} copy(bf16[1,64,81,512]{3,1,2,0:T(8,128)(2,1)} %param.13) | data formatting | bytes 10616832 | tf_op args[5]
  23.2 29.4 %feature_path.1 = (bf16[64,176,512]{2,1,0:T(8,128)(2,1)}, f32[64,16,81]{2,1,0:T(8,128)}, bf16[64,16,81]{2,1,0:T(8,128)(2,1)}, bf16[64,16,81]{2,1,0:T(8,128)(2,1)...) custom-call(bf16[64,81,512]{2,1,0:T(8,128)(2,1)} %bitcast.29, bf16[64,176,16]{2,1,0:T(8,128)(2,1)} %copy.13.wt_ref, ...), custom_call_target="tpu_custom_call" | custom-call | flops 10240000000 | bytes 16000000 | tf_op jit(solution)/shard_map/feature_path/pallas_call | solution.py:111
  52.6 2.0 %collective-permute-start = (bf16[64,16,81]{2,1,0:T(8,128)(2,1)}, bf16[64,16,81]{2,1,0:T(8,128)(2,1)S(1)}, u32[]{:S(2)}, u32[]{:S(2)}) collective-permute-start(bf16[64,16,81]{2,1,0:T(8,128)(2,1)} %get-tuple-element.14), channel_id=1, source_target_pairs={{0,24},{4,28},{8,0},{12,4},{16,8},{20,12},{24,16},{28,20},{1,25},{... | collective-permute-start | bytes 497672 | tf_op jit(solution)/shard_map/ppermute | solution.py:40
  54.6 0.5 collective-permute-start.1
  55.1 1.5 %collective-permute-start.2 = (bf16[64,16,81]{2,1,0:T(8,128)(2,1)}, bf16[64,16,81]{2,1,0:T(8,128)(2,1)S(1)}, u32[]{:S(2)}, u32[]{:S(2)}) collective-permute-start(bf16[64,16,81]{2,1,0:T(8,128)(2,1)} %get-tuple-element.16), channel_id=1, source_target_pairs={{0,4},{4,8},{8,12},{12,16},{16,20},{20,24},{24,28},{28,0},{1,5},{5... | collective-permute-start | bytes 497672 | tf_op jit(solution)/shard_map/ppermute | solution.py:40
  56.8 0.6 copy-done.9
  57.3 0.1 copy-done.10
  57.5 29.3 %filter_path.1 = (f32[8,512]{1,0:T(8,128)}, f32[64,8,81]{2,1,0:T(8,128)}) custom-call(bf16[64,176,512]{2,1,0:T(8,128)(2,1)} %get-tuple-element.18.grid_ref, bf16[64,16,176]{2,1,0:T(8,128)(2,1)} %get-tuple-element.23.wt_ref, bf16[80,512]{1,0:T(8,128)(2,1)} %fusion.2.sel_ref, bf16[16,512]{1,0:T(8,128)(2,1)} %pad_maximum_fusion.1.rad_ref, ...), custom_call_target="tpu_custom_call" | custom-call | flops 10240000000 | bytes 16000000 | tf_op jit(solution)/shard_map/filter_path/pallas_call | solution.py:111
  86.7 0.9 copy-done.1
  87.7 0.7 copy-done.2
  88.4 18.7 %sums.1 = (f32[16,32,81]{2,1,0:T(8,128)S(1)}, f32[8,512]{1,0:T(8,128)S(1)}) custom-call(f32[16,32,81]{2,1,0:T(8,128)S(1)} %bitcast.27, f32[8,512]{1,0:T(8,128)S(1)} %copy-done.2), custom_call_target="tpu_custom_call" | custom-call | tf_op jit(solution)/shard_map/sums/pallas_call | solution.py:226
  107.2 0.8 copy.20
  108.0 0.9 add_bitcast_fusion
  108.9 0.6 copy.22
  (34 shorter events, 0.5 us)
Async XLA Ops:
  0.6 8.1 %copy-start = (bf16[8,64,81]{2,1,0:T(8,128)(2,1)S(1)}, bf16[8,64,81]{2,1,0:T(8,128)(2,1)}, u32[]{:S(2)}) copy-start(bf16[8,64,81]{2,1,0:T(8,128)(2,1)} %param.12) | copy-start | bytes 248836
  0.6 13.0 %copy-start.6 = (s32[1,16]{1,0:T(1,128)S(1)}, s32[1,16]{1,0:T(1,128)}, u32[]{:S(2)}) copy-start(s32[1,16]{1,0:T(1,128)} %param.10) | copy-start | bytes 196
  0.7 13.2 %copy-start.4 = (s32[1,16,32]{2,1,0:T(8,128)S(1)}, s32[1,16,32]{2,1,0:T(8,128)}, u32[]{:S(2)}) copy-start(s32[1,16,32]{2,1,0:T(8,128)} %param.9) | copy-start | bytes 6148
  0.7 13.9 %copy-start.5 = (bf16[1,8,512]{2,1,0:T(8,128)(2,1)S(1)}, bf16[1,8,512]{2,1,0:T(8,128)(2,1)}, u32[]{:S(2)}) copy-start(bf16[1,8,512]{2,1,0:T(8,128)(2,1)} %param.11) | copy-start | bytes 24580
  0.7 53.9 %collective-permute-start.4 = (bf16[64,16,81]{2,1,0:T(8,128)(2,1)}, bf16[64,16,81]{2,1,0:T(8,128)(2,1)S(1)}, u32[]{:S(2)}, u32[]{:S(2)}) collective-permute-start(bf16[64,16,81]{2,1,0:T(8,128)(2,1)} %bitcast.33), channel_id=1, source_target_pairs={{0,8},{4,12},{8,16},{12,20},{16,24},{20,28},{24,0},{28,4},{1,9},{5... | collective-permute-start | bytes 497672 | tf_op jit(solution)/shard_map/ppermute | solution.py:40
  3.8 51.3 %collective-permute-start.5 = (bf16[64,16,81]{2,1,0:T(8,128)(2,1)}, bf16[64,16,81]{2,1,0:T(8,128)(2,1)S(1)}, u32[]{:S(2)}, u32[]{:S(2)}) collective-permute-start(bf16[64,16,81]{2,1,0:T(8,128)(2,1)} %bitcast.34), channel_id=1, source_target_pairs={{0,4},{4,8},{8,12},{12,16},{16,20},{20,24},{24,28},{28,0},{1,5},{5... | collective-permute-start | bytes 497672 | tf_op jit(solution)/shard_map/ppermute | solution.py:40
  5.2 51.4 %collective-permute-start.6 = (bf16[64,16,81]{2,1,0:T(8,128)(2,1)}, bf16[64,16,81]{2,1,0:T(8,128)(2,1)S(1)}, u32[]{:S(2)}, u32[]{:S(2)}) collective-permute-start(bf16[64,16,81]{2,1,0:T(8,128)(2,1)} %bitcast.35), channel_id=1, source_target_pairs={{0,28},{4,0},{8,4},{12,8},{16,12},{20,16},{24,20},{28,24},{1,29},{... | collective-permute-start | bytes 497672 | tf_op jit(solution)/shard_map/ppermute | solution.py:40
  8.5 48.3 %collective-permute-start.7 = (bf16[64,16,81]{2,1,0:T(8,128)(2,1)}, bf16[64,16,81]{2,1,0:T(8,128)(2,1)S(1)}, u32[]{:S(2)}, u32[]{:S(2)}) collective-permute-start(bf16[64,16,81]{2,1,0:T(8,128)(2,1)} %bitcast.36), channel_id=1, source_target_pairs={{0,24},{4,28},{8,0},{12,4},{16,8},{20,12},{24,16},{28,20},{1,25},{... | collective-permute-start | bytes 497672 | tf_op jit(solution)/shard_map/ppermute | solution.py:40
  52.6 55.3 %collective-permute-start = (bf16[64,16,81]{2,1,0:T(8,128)(2,1)}, bf16[64,16,81]{2,1,0:T(8,128)(2,1)S(1)}, u32[]{:S(2)}, u32[]{:S(2)}) collective-permute-start(bf16[64,16,81]{2,1,0:T(8,128)(2,1)} %get-tuple-element.14), channel_id=1, source_target_pairs={{0,24},{4,28},{8,0},{12,4},{16,8},{20,12},{24,16},{28,20},{1,25},{... | collective-permute-start | bytes 497672 | tf_op jit(solution)/shard_map/ppermute | solution.py:40
  54.6 2.2 %copy-start.7 = (bf16[64,16,81]{2,1,0:T(8,128)(2,1)}, bf16[64,16,81]{2,1,0:T(8,128)(2,1)S(1)}, u32[]{:S(2)}) copy-start(bf16[64,16,81]{2,1,0:T(8,128)(2,1)S(1)} %collective-permute-done.4.refs_0_) | copy-start | bytes 497668
  54.6 53.3 %collective-permute-start.1 = (bf16[64,16,81]{2,1,0:T(8,128)(2,1)}, bf16[64,16,81]{2,1,0:T(8,128)(2,1)S(1)}, u32[]{:S(2)}, u32[]{:S(2)}) collective-permute-start(bf16[64,16,81]{2,1,0:T(8,128)(2,1)} %get-tuple-element.15), channel_id=1, source_target_pairs={{0,28},{4,0},{8,4},{12,8},{16,12},{20,16},{24,20},{28,24},{1,29},{... | collective-permute-start | bytes 497672 | tf_op jit(solution)/shard_map/ppermute | solution.py:40
  55.1 1.7 %copy-start.8 = (bf16[64,16,81]{2,1,0:T(8,128)(2,1)}, bf16[64,16,81]{2,1,0:T(8,128)(2,1)S(1)}, u32[]{:S(2)}) copy-start(bf16[64,16,81]{2,1,0:T(8,128)(2,1)S(1)} %collective-permute-done.5.refs_1_) | copy-start | bytes 497668
  55.1 52.9 %collective-permute-start.2 = (bf16[64,16,81]{2,1,0:T(8,128)(2,1)}, bf16[64,16,81]{2,1,0:T(8,128)(2,1)S(1)}, u32[]{:S(2)}, u32[]{:S(2)}) collective-permute-start(bf16[64,16,81]{2,1,0:T(8,128)(2,1)} %get-tuple-element.16), channel_id=1, source_target_pairs={{0,4},{4,8},{8,12},{12,16},{16,20},{20,24},{24,28},{28,0},{1,5},{5... | collective-permute-start | bytes 497672 | tf_op jit(solution)/shard_map/ppermute | solution.py:40
  56.6 0.7 copy-start.9
  56.6 51.3 %collective-permute-start.3 = (bf16[64,16,81]{2,1,0:T(8,128)(2,1)}, bf16[64,16,81]{2,1,0:T(8,128)(2,1)S(1)}, u32[]{:S(2)}, u32[]{:S(2)}) collective-permute-start(bf16[64,16,81]{2,1,0:T(8,128)(2,1)} %get-tuple-element.17), channel_id=1, source_target_pairs={{0,8},{4,12},{8,16},{12,20},{16,24},{20,28},{24,0},{28,4},{1,9},{5... | collective-permute-start | bytes 497672 | tf_op jit(solution)/shard_map/ppermute | solution.py:40
  56.8 0.7 copy-start.10
  57.5 50.5 %copy-start.3 = (f32[64,16,81]{2,1,0:T(8,128)S(1)}, f32[64,16,81]{2,1,0:T(8,128)}, u32[]{:S(2)}) copy-start(f32[64,16,81]{2,1,0:T(8,128)} %get-tuple-element.13) | copy-start | bytes 995332
  86.7 0.9 copy-start.1
  87.7 0.7 copy-start.2

commit v3 on v2

--- a/solution.py
+++ b/solution.py
@@ -16,7 +16,9 @@
 REACH = 2
 G = 81
 G_PAD = 96
-GROUP = 4
+GROUP = 16
+SUB = 4
+LANES = 128
 
 
 def basis_table():
@@ -44,58 +46,101 @@
     return lax.dot_general(a, b, (contract, ((), ())), preferred_element_type=jnp.float32)
 
 
+def split_parts(value, axis):
+    half = value.shape[axis] // 2
+    coarse = value.astype(jnp.bfloat16).astype(jnp.float32)
+    index = lax.broadcasted_iota(jnp.int32, value.shape, axis)
+    return jnp.where(index < half, coarse, value - coarse).astype(jnp.bfloat16)
+
+
 def feature_kernel(
-    grad_ref, wt_ref, sel_ref, rad_ref, table_ref, rows_ref, grid_ref, own_ref, *sent_refs
+    weight_ref, grad_ref, sel_ref, rad_ref, table_ref, rows_ref, grid_ref, own_ref, *refs
 ):
     bf16 = jnp.bfloat16
-    sel = sel_ref[...]
-    rad = rad_ref[...]
-    table = table_ref[...]
+    sent_refs, spread = refs[:-1], refs[-1]
     rows = rows_ref[...]
     block_len = own_ref.shape[1]
-    for c in range(GROUP):
-        weighted = dot(rows, grad_ref[c])
-        filt_grid = dot(wt_ref[c], rad)
-        grid_ref[c] = weighted.astype(bf16)
-        feat_side = (weighted * filt_grid).astype(bf16)
-        edge_grad = dot(table, feat_side).astype(bf16)
-        placed = (dot(sel, edge_grad, ((1,), (1,))) * (1.0 / SAMPLES))[:, :G]
-        blocks = [
-            placed[index * block_len : (index + 1) * block_len] for index in range(2 * REACH + 1)
+    for tile in range(spread.shape[0]):
+        spread[tile] = (
+            grad_ref[:, :, tile * LANES : (tile + 1) * LANES]
+            .astype(jnp.float32)
+            .reshape(spread.shape[1:])
+        )
+
+    @pl.loop(0, GROUP // SUB)
+    def _(batch):
+        first = batch * SUB
+        filters = [
+            split_parts(dot(rows, weight_ref[first + c], ((1,), (1,))), 1) for c in range(SUB)
         ]
-        own_ref[c] = blocks.pop(REACH)
-        for sent_ref, block in zip(sent_refs, blocks):
-            sent_ref[c] = block.astype(bf16)
+        filt_grid = dot(jnp.concatenate(filters, axis=0), rad_ref[...])
+        sides = []
+        for c in range(SUB):
+            grad = jnp.concatenate(
+                [
+                    spread[tile, pl.ds(first + c, G, stride=GROUP), :].astype(bf16)
+                    for tile in range(spread.shape[0])
+                ],
+                axis=1,
+            )
+            weighted = dot(rows, grad)
+            grid_ref[first + c] = weighted.astype(bf16)
+            sides.append(
+                (weighted * filt_grid[c * SAMPLES_PAD : (c + 1) * SAMPLES_PAD]).astype(bf16)
+            )
+        summed = dot(jnp.concatenate(sides, axis=0), sel_ref[...]).astype(bf16)
+        for c in range(SUB):
+            placed = dot(table_ref[...], summed[c * SAMPLES_PAD : (c + 1) * SAMPLES_PAD])
+            placed = (placed.T * (1.0 / SAMPLES))[:, :G]
+            blocks = [
+                placed[index * block_len : (index + 1) * block_len]
+                for index in range(2 * REACH + 1)
+            ]
+            own_ref[first + c] = blocks.pop(REACH)
+            for sent_ref, block in zip(sent_refs, blocks):
+                sent_ref[first + c] = block.astype(bf16)
 
 
 def filter_kernel(
-    grid_ref, wt_ref, sel_ref, rad_ref, table_ref, rows_ref, *refs
+    weight_ref, grid_ref, sel_ref, rad_ref, table_ref, rows_ref, rows_rest_ref, cols_ref, *refs
 ):
     bf16 = jnp.bfloat16
-    window_refs, (radial_ref, weight_ref) = refs[:-2], refs[-2:]
+    window_refs, (radial_ref, out_ref) = refs[:-2], refs[-2:]
+    basis_count = radial_ref.shape[0]
 
     @pl.when(pl.program_id(0) == 0)
     def _():
         radial_ref[...] = jnp.zeros_like(radial_ref)
 
-    sel = sel_ref[...]
-    table = table_ref[...]
-    rows = rows_ref[...]
-    basis_count = radial_ref.shape[0]
-    rad = rad_ref[:basis_count]
-    radial_sum = jnp.zeros(radial_ref.shape, jnp.float32)
-    for c in range(GROUP):
-        window = jnp.concatenate([ref[c] for ref in window_refs], axis=0)
-        atom_grid = dot(rows, window, ((1,), (1,))).astype(bf16)
-        feat_grid = dot(atom_grid, sel)
-        filt_side = (grid_ref[c].astype(jnp.float32) * feat_grid).astype(bf16)
-        both = dot(jnp.concatenate([table, wt_ref[c]], axis=0), filt_side)
-        filt_grad = both[:G_PAD].astype(bf16)
-        radial_sum = (
-            radial_sum + both[G_PAD : G_PAD + basis_count] + both[G_PAD + basis_count :]
-        )
-        weight_ref[c] = dot(rad, filt_grad, ((1,), (1,)))[:, :G]
-    radial_ref[...] += radial_sum
+    @pl.loop(0, GROUP // SUB)
+    def _(batch):
+        first = batch * SUB
+        atom_grids = []
+        for c in range(SUB):
+            window = jnp.concatenate([ref[first + c] for ref in window_refs], axis=0)
+            atom_grids.append(
+                (
+                    dot(rows_ref[...], window, ((1,), (1,)))
+                    + dot(rows_rest_ref[...], window, ((1,), (1,)))
+                ).astype(bf16)
+            )
+        feat_grid = dot(jnp.concatenate(atom_grids, axis=0), sel_ref[...])
+        sides = [
+            (
+                grid_ref[first + c].astype(jnp.float32)
+                * feat_grid[c * SAMPLES_PAD : (c + 1) * SAMPLES_PAD]
+            ).astype(bf16)
+            for c in range(SUB)
+        ]
+        summed = dot(jnp.concatenate(sides, axis=0), rad_ref[...]).astype(bf16)
+        radial_sum = radial_ref[...]
+        for c in range(SUB):
+            filters = split_parts(dot(weight_ref[first + c], cols_ref[...]), 0)
+            parts = dot(filters, sides[c])
+            radial_sum = radial_sum + parts[:basis_count] + parts[basis_count:]
+            placed = dot(table_ref[...], summed[c * SAMPLES_PAD : (c + 1) * SAMPLES_PAD])
+            out_ref[first + c] = placed.T[:, :G]
+        radial_ref[...] = radial_sum
 
 
 def whole(x):
@@ -106,22 +151,24 @@
     return pl.BlockSpec((GROUP,) + tuple(shape), lambda i: (i, 0, 0))
 
 
-def grid_call(kernel, name, out_shape, out_specs, split, shared, split_last=()):
+def grid_call(kernel, name, out_shape, out_specs, split, special, shared, split_last=(), scratch=()):
     chan_count = split[0].shape[0]
     return pl.pallas_call(
         kernel,
         grid=(chan_count // GROUP,),
         in_specs=[grouped(x.shape[1:]) for x in split]
+        + [spec for _, spec in special]
         + [whole(x) for x in shared]
         + [grouped(x.shape[1:]) for x in split_last],
         out_specs=out_specs,
         out_shape=out_shape,
+        scratch_shapes=list(scratch),
         compiler_params=pltpu.CompilerParams(vmem_limit_bytes=54 * 1024 * 1024),
         cost_estimate=pl.CostEstimate(
             flops=chan_count * 160_000_000, bytes_accessed=16_000_000, transcendentals=0
         ),
         name=name,
-    )(*split, *shared, *split_last)
+    )(*split, *[x for x, _ in special], *shared, *split_last)
 
 
 def sum_kernel(
@@ -246,7 +293,8 @@
 def local(feats, neighbors, counts, radial, filter_weight, message_grad):
     exact = basis_table()
     table = jnp.asarray(exact, jnp.bfloat16)
-    rows = jnp.asarray(exact[:G].T, jnp.bfloat16)
+    rows_np = exact[:G].T.astype(jnp.bfloat16)
+    rows = jnp.asarray(rows_np)
     atom_count = lax.axis_size("atom")
     position = lax.axis_index("atom")
     block_len = feats.shape[3]
@@ -263,16 +311,14 @@
         sources // block_len - position + REACH
     ) % atom_count * block_len + sources % block_len
     valid = (jnp.arange(SLOTS, dtype=jnp.int32)[None, :] < counts[0][:, None]).reshape(-1)
-    selector = (
-        (slot_index[None, :] == jnp.arange(window_len, dtype=jnp.int32)[:, None]) & valid[None, :]
-    ).astype(jnp.bfloat16)
+    slots = jnp.arange(window_len, dtype=jnp.int32)
+    selector = ((slot_index[None, :] == slots[:, None]) & valid[None, :]).astype(jnp.bfloat16)
+    selector_rows = ((slot_index[:, None] == slots[None, :]) & valid[:, None]).astype(jnp.bfloat16)
     radial_e = radial[0] * valid.astype(jnp.bfloat16)[None, :]
     radial_twice = jnp.concatenate([radial_e, radial_e], axis=0)
-    weight_grid = jnp.einsum(
-        "kcg,gp->ckp", filter_weight, table[:G], preferred_element_type=jnp.float32
-    )
-    coarse = lax.reduce_precision(weight_grid, 8, 7)
-    weight_parts = jnp.concatenate([coarse, weight_grid - coarse], axis=1).astype(jnp.bfloat16)
+    rows_rest = jnp.asarray(exact[:G].T - np.asarray(rows_np, np.float32), jnp.bfloat16)
+    weight_c = jnp.transpose(filter_weight, (1, 0, 2))
+    weight_twice = jnp.concatenate([weight_c, weight_c], axis=1)
     basis_count = radial_e.shape[0]
     edges = radial_e.shape[1]
     block_shape = (chan_count, block_len, G)
@@ -285,8 +331,15 @@
         ]
         + [jax.ShapeDtypeStruct(block_shape, jnp.bfloat16)] * (2 * REACH),
         [grouped((SAMPLES_PAD, edges))] + [grouped(block_shape[1:])] * (2 * REACH + 1),
-        [message_grad[0], jnp.transpose(weight_parts, (0, 2, 1))],
-        [selector, radial_twice, table, rows],
+        [weight_twice],
+        [
+            (
+                jnp.transpose(message_grad[0], (1, 0, 2)),
+                pl.BlockSpec((G, GROUP, edges), lambda i: (0, i, 0)),
+            )
+        ],
+        [selector_rows, radial_twice, table, rows],
+        scratch=[pltpu.VMEM((edges // LANES, G * GROUP, LANES), jnp.float32)],
     )
     arrived = [
         passed_along(block, "atom", offset)
@@ -303,8 +356,9 @@
             pl.BlockSpec((basis_count, edges), lambda i: (0, 0)),
             grouped((basis_count, G)),
         ],
-        [grid, weight_parts],
-        [selector, radial_twice, table, rows],
+        [weight_twice, grid],
+        [],
+        [selector, radial_e.T, table, rows, rows_rest, table[:G]],
         window,
     )
     sharers = atom_count * lax.axis_size("rep")

time: 110 us -> 99.2 us (0.902)
  local copies, waits for them, and re-layouts: 14.6 us -> 6.5 us
  Pallas kernels: 77.4 us -> 71.1 us
  starting transfers between devices: 12.2 us -> 14.9 us
  other arithmetic: 3.54 us -> 5.55 us
    unnamed x24 -> x17, local copies, waits for them, and re-layouts: 11 us -> 4.82 us
    pallas_call x2, Pallas kernels: 58.7 us -> 53.7 us  [grid_call(): pl.pallas_call(kernel, grid=(chan_count // GROUP,), in_specs=[grouped(x.s...]
    transpose x1 -> x0, local copies, waits for them, and re-layouts: 2.67 us -> none  [local(): jnp.transpose(weight_parts, (0, 2, 1))]
    ppermute x8, starting transfers between devices: 12.2 us -> 14.9 us  [passed_along(): return lax.ppermute(value, axis, pairs)]
    pallas_call x1, Pallas kernels: 18.7 us -> 17.4 us  [sum_call(): pl.pallas_call(sum_kernel, in_specs=[vmem, vmem], out_specs=[vmem, vmem],...]
  transfers between devices with their start and end apart: 8 -> 8, of which waited for: 0 -> 0; matrix products, arithmetic and copies ran while one was open for 14% -> 8% of each run, Pallas kernels for 71% -> 72%
where the time goes in v3:
time: 99.2 us; the launch traced here: 98.8 us
  Pallas kernels  71.1 us (72%)
  starting transfers between devices  14.9 us (15%)
  local copies, waits for them, and re-layouts  6.5 us (7%)
  other arithmetic  5.55 us (6%)
    pallas_call x2, Pallas kernels, grid_call(): pl.pallas_call(kernel, grid=(chan_count // GROUP,), in_specs=[grouped(x.s...  53.7 us
    pallas_call x1, Pallas kernels, sum_call(): pl.pallas_call(sum_kernel, in_specs=[vmem, vmem], out_specs=[vmem, vmem],...  17.4 us
    ppermute x8, starting transfers between devices, passed_along(): return lax.ppermute(value, axis, pairs)  14.9 us
    unnamed x17, local copies, waits for them, and re-layouts  4.82 us
  transfers between devices with their start and end apart: 8, of which 0 were waited for; matrix products, arithmetic and copies ran while one was open for 8% of the time, Pallas kernels for 72%

profile of v3, /device:TPU:0, one launch (start us, length us, event | category | flops | bytes accessed | tf_op | source)
XLA Modules:
  0.0 98.8 jit_solution(2633115821794106108)
XLA Ops:
  0.6 3.1 %collective-permute-start.4 = (bf16[64,16,81]{2,1,0:T(8,128)(2,1)}, bf16[64,16,81]{2,1,0:T(8,128)(2,1)S(1)}, u32[]{:S(2)}, u32[]{:S(2)}) collective-permute-start(bf16[64,16,81]{2,1,0:T(8,128)(2,1)} %bitcast.33), channel_id=1, source_target_pairs={{0,8},{4,12},{8,16},{12,20},{16,24},{20,28},{24,0},{28,4},{1,9},{5... | collective-permute-start | bytes 497672 | tf_op jit(solution)/shard_map/ppermute | solution.py:42
  3.7 1.5 %collective-permute-start.5 = (bf16[64,16,81]{2,1,0:T(8,128)(2,1)}, bf16[64,16,81]{2,1,0:T(8,128)(2,1)S(1)}, u32[]{:S(2)}, u32[]{:S(2)}) collective-permute-start(bf16[64,16,81]{2,1,0:T(8,128)(2,1)} %bitcast.34), channel_id=1, source_target_pairs={{0,4},{4,8},{8,12},{12,16},{16,20},{20,24},{24,28},{28,0},{1,5},{5... | collective-permute-start | bytes 497672 | tf_op jit(solution)/shard_map/ppermute | solution.py:42
  5.2 3.2 %collective-permute-start.6 = (bf16[64,16,81]{2,1,0:T(8,128)(2,1)}, bf16[64,16,81]{2,1,0:T(8,128)(2,1)S(1)}, u32[]{:S(2)}, u32[]{:S(2)}) collective-permute-start(bf16[64,16,81]{2,1,0:T(8,128)(2,1)} %bitcast.35), channel_id=1, source_target_pairs={{0,28},{4,0},{8,4},{12,8},{16,12},{20,16},{24,20},{28,24},{1,29},{... | collective-permute-start | bytes 497672 | tf_op jit(solution)/shard_map/ppermute | solution.py:42
  8.4 0.3 collective-permute-start.7
  8.7 1.0 %copy.24 = bf16[8,64,81]{2,0,1:T(8,128)(2,1)S(1)} copy(bf16[8,64,81]{2,1,0:T(8,128)(2,1)} %param.13) | data formatting | bytes 165888 | tf_op args[4]
  9.7 0.8 pad_maximum_fusion.weight_ref
  10.5 0.8 reshape_squeeze.3
  11.3 0.7 iota_compare_fusion.2
  12.1 0.9 fusion.1.sel_ref
  13.0 0.9 copy.17
  14.0 0.6 pad_maximum_fusion.1.rad_ref
  14.7 22.7 %feature_path.1 = (bf16[64,176,512]{2,1,0:T(8,128)(2,1)}, f32[64,16,81]{2,1,0:T(8,128)}, bf16[64,16,81]{2,1,0:T(8,128)(2,1)}, bf16[64,16,81]{2,1,0:T(8,128)(2,1)...) custom-call(bf16[64,16,81]{2,1,0:T(8,128)(2,1)} %pad_maximum_fusion.weight_ref, ...), custom_call_target="tpu_custom_call" | custom-call | flops 10240000000 | bytes 16000000 | tf_op jit(solution)/shard_map/feature_path/pallas_call | solution.py:156
  37.3 1.8 %collective-permute-start.3 = (bf16[64,16,81]{2,1,0:T(8,128)(2,1)}, bf16[64,16,81]{2,1,0:T(8,128)(2,1)S(1)}, u32[]{:S(2)}, u32[]{:S(2)}) collective-permute-start(bf16[64,16,81]{2,1,0:T(8,128)(2,1)} %get-tuple-element.17), channel_id=1, source_target_pairs={{0,8},{4,12},{8,16},{12,20},{16,24},{20,28},{24,0},{28,4},{1,9},{5... | collective-permute-start | bytes 497672 | tf_op jit(solution)/shard_map/ppermute | solution.py:42
  39.1 0.8 fusion.10.rad_ref
  39.9 0.7 fusion.3.sel_ref
  40.6 4.7 %collective-permute-start.1 = (bf16[64,16,81]{2,1,0:T(8,128)(2,1)}, bf16[64,16,81]{2,1,0:T(8,128)(2,1)S(1)}, u32[]{:S(2)}, u32[]{:S(2)}) collective-permute-start(bf16[64,16,81]{2,1,0:T(8,128)(2,1)} %get-tuple-element.15), channel_id=1, source_target_pairs={{0,28},{4,0},{8,4},{12,8},{16,12},{20,16},{24,20},{28,24},{1,29},{... | collective-permute-start | bytes 497672 | tf_op jit(solution)/shard_map/ppermute | solution.py:42
  45.6 0.4 copy-done.5
  46.3 31.0 %filter_path.1 = (f32[8,512]{1,0:T(8,128)}, f32[64,8,81]{2,1,0:T(8,128)}) custom-call(bf16[64,16,81]{2,1,0:T(8,128)(2,1)} %pad_maximum_fusion.weight_ref, bf16[64,176,512]{2,1,0:T(8,128)(2,1)} %get-tuple-element.18.grid_ref, bf16[80,512]{1,0:T(8,128)(2,1)} %fusion.3.sel_ref, bf16[512,8]{1,0:T(8,128)(2,1)} %fusion.10.rad_ref, ...), custom_call_target="tpu_custom_call" | custom-call | flops 10240000000 | bytes 16000000 | tf_op jit(solution)/shard_map/filter_path/pallas_call | solution.py:156
  77.3 0.9 copy-done
  78.3 0.7 copy-done.1
  79.0 17.4 %sums.1 = (f32[16,32,81]{2,1,0:T(8,128)S(1)}, f32[8,512]{1,0:T(8,128)S(1)}) custom-call(f32[16,32,81]{2,1,0:T(8,128)S(1)} %bitcast.26, f32[8,512]{1,0:T(8,128)S(1)} %copy-done.1), custom_call_target="tpu_custom_call" | custom-call | tf_op jit(solution)/shard_map/sums/pallas_call | solution.py:273
  96.5 0.8 copy.23
  97.3 0.9 add_bitcast_fusion
  98.2 0.6 copy.26
  (27 shorter events, 1.0 us)
Async XLA Ops:
  0.6 39.9 %collective-permute-start.4 = (bf16[64,16,81]{2,1,0:T(8,128)(2,1)}, bf16[64,16,81]{2,1,0:T(8,128)(2,1)S(1)}, u32[]{:S(2)}, u32[]{:S(2)}) collective-permute-start(bf16[64,16,81]{2,1,0:T(8,128)(2,1)} %bitcast.33), channel_id=1, source_target_pairs={{0,8},{4,12},{8,16},{12,20},{16,24},{20,28},{24,0},{28,4},{1,9},{5... | collective-permute-start | bytes 497672 | tf_op jit(solution)/shard_map/ppermute | solution.py:42
  3.7 36.9 %collective-permute-start.5 = (bf16[64,16,81]{2,1,0:T(8,128)(2,1)}, bf16[64,16,81]{2,1,0:T(8,128)(2,1)S(1)}, u32[]{:S(2)}, u32[]{:S(2)}) collective-permute-start(bf16[64,16,81]{2,1,0:T(8,128)(2,1)} %bitcast.34), channel_id=1, source_target_pairs={{0,4},{4,8},{8,12},{12,16},{16,20},{20,24},{24,28},{28,0},{1,5},{5... | collective-permute-start | bytes 497672 | tf_op jit(solution)/shard_map/ppermute | solution.py:42
  5.2 40.1 %collective-permute-start.6 = (bf16[64,16,81]{2,1,0:T(8,128)(2,1)}, bf16[64,16,81]{2,1,0:T(8,128)(2,1)S(1)}, u32[]{:S(2)}, u32[]{:S(2)}) collective-permute-start(bf16[64,16,81]{2,1,0:T(8,128)(2,1)} %bitcast.35), channel_id=1, source_target_pairs={{0,28},{4,0},{8,4},{12,8},{16,12},{20,16},{24,20},{28,24},{1,29},{... | collective-permute-start | bytes 497672 | tf_op jit(solution)/shard_map/ppermute | solution.py:42
  8.4 37.2 %collective-permute-start.7 = (bf16[64,16,81]{2,1,0:T(8,128)(2,1)}, bf16[64,16,81]{2,1,0:T(8,128)(2,1)S(1)}, u32[]{:S(2)}, u32[]{:S(2)}) collective-permute-start(bf16[64,16,81]{2,1,0:T(8,128)(2,1)} %bitcast.36), channel_id=1, source_target_pairs={{0,24},{4,28},{8,0},{12,4},{16,8},{20,12},{24,16},{28,20},{1,25},{... | collective-permute-start | bytes 497672 | tf_op jit(solution)/shard_map/ppermute | solution.py:42
  37.3 59.9 %collective-permute-start.3 = (bf16[64,16,81]{2,1,0:T(8,128)(2,1)}, bf16[64,16,81]{2,1,0:T(8,128)(2,1)S(1)}, u32[]{:S(2)}, u32[]{:S(2)}) collective-permute-start(bf16[64,16,81]{2,1,0:T(8,128)(2,1)} %get-tuple-element.17), channel_id=1, source_target_pairs={{0,8},{4,12},{8,16},{12,20},{16,24},{20,28},{24,0},{28,4},{1,9},{5... | collective-permute-start | bytes 497672 | tf_op jit(solution)/shard_map/ppermute | solution.py:42
  40.6 5.0 %copy-start.3 = (bf16[64,16,81]{2,1,0:T(8,128)(2,1)}, bf16[64,16,81]{2,1,0:T(8,128)(2,1)S(1)}, u32[]{:S(2)}) copy-start(bf16[64,16,81]{2,1,0:T(8,128)(2,1)S(1)} %collective-permute-done.4.refs_0_) | copy-start | bytes 497668
  40.6 56.6 %collective-permute-start.2 = (bf16[64,16,81]{2,1,0:T(8,128)(2,1)}, bf16[64,16,81]{2,1,0:T(8,128)(2,1)S(1)}, u32[]{:S(2)}, u32[]{:S(2)}) collective-permute-start(bf16[64,16,81]{2,1,0:T(8,128)(2,1)} %get-tuple-element.16), channel_id=1, source_target_pairs={{0,4},{4,8},{8,12},{12,16},{16,20},{20,24},{24,28},{28,0},{1,5},{5... | collective-permute-start | bytes 497672 | tf_op jit(solution)/shard_map/ppermute | solution.py:42
  40.6 5.0 %copy-start.4 = (bf16[64,16,81]{2,1,0:T(8,128)(2,1)}, bf16[64,16,81]{2,1,0:T(8,128)(2,1)S(1)}, u32[]{:S(2)}) copy-start(bf16[64,16,81]{2,1,0:T(8,128)(2,1)S(1)} %collective-permute-done.5.refs_1_) | copy-start | bytes 497668
  40.6 56.6 %collective-permute-start.1 = (bf16[64,16,81]{2,1,0:T(8,128)(2,1)}, bf16[64,16,81]{2,1,0:T(8,128)(2,1)S(1)}, u32[]{:S(2)}, u32[]{:S(2)}) collective-permute-start(bf16[64,16,81]{2,1,0:T(8,128)(2,1)} %get-tuple-element.15), channel_id=1, source_target_pairs={{0,28},{4,0},{8,4},{12,8},{16,12},{20,16},{24,20},{28,24},{1,29},{... | collective-permute-start | bytes 497672 | tf_op jit(solution)/shard_map/ppermute | solution.py:42
  45.3 0.7 copy-start.5
  45.3 51.9 %collective-permute-start = (bf16[64,16,81]{2,1,0:T(8,128)(2,1)}, bf16[64,16,81]{2,1,0:T(8,128)(2,1)S(1)}, u32[]{:S(2)}, u32[]{:S(2)}) collective-permute-start(bf16[64,16,81]{2,1,0:T(8,128)(2,1)} %get-tuple-element.14), channel_id=1, source_target_pairs={{0,24},{4,28},{8,0},{12,4},{16,8},{20,12},{24,16},{28,20},{1,25},{... | collective-permute-start | bytes 497672 | tf_op jit(solution)/shard_map/ppermute | solution.py:42
  45.6 0.7 copy-start.6
  46.3 50.9 %copy-start.2 = (f32[64,16,81]{2,1,0:T(8,128)S(1)}, f32[64,16,81]{2,1,0:T(8,128)}, u32[]{:S(2)}) copy-start(f32[64,16,81]{2,1,0:T(8,128)} %get-tuple-element.13) | copy-start | bytes 995332
  77.3 0.9 copy-start
  78.3 0.7 copy-start.1

commit v4 on v3

--- a/solution.py
+++ b/solution.py
@@ -46,54 +46,94 @@
     return lax.dot_general(a, b, (contract, ((), ())), preferred_element_type=jnp.float32)
 
 
-def split_parts(value, axis):
-    half = value.shape[axis] // 2
+def fill_filters(weight_ref, cols_ref, filt_rows):
+    basis_count, group, coefficients = weight_ref.shape
+    rows = dot(weight_ref[...].reshape(basis_count * group, coefficients), cols_ref[...])
+    for half in range(filt_rows.shape[0]):
+        filt_rows[half] = rows[:, half * LANES : (half + 1) * LANES]
+
+
+def filters_of(filt_rows, channel):
+    halves = [
+        filt_rows[half, pl.ds(channel, filt_rows.shape[1] // GROUP, stride=GROUP), :]
+        for half in range(filt_rows.shape[0])
+    ]
+    value = jnp.concatenate(halves, axis=1)
     coarse = value.astype(jnp.bfloat16).astype(jnp.float32)
-    index = lax.broadcasted_iota(jnp.int32, value.shape, axis)
-    return jnp.where(index < half, coarse, value - coarse).astype(jnp.bfloat16)
+    return jnp.concatenate([coarse, value - coarse], axis=0)
+
+
+def selector(code_ref):
+    code = code_ref[...]
+    place = lax.broadcasted_iota(jnp.int32, (LANES, code.shape[1]), 0)
+    return jnp.where(place == code, 1.0, 0.0)
+
+
+def masked_radial(code_ref, rad_ref):
+    return jnp.where(code_ref[...] >= 0, rad_ref[...].astype(jnp.float32), 0.0)
 
 
 def feature_kernel(
-    weight_ref, grad_ref, sel_ref, rad_ref, table_ref, rows_ref, grid_ref, own_ref, *refs
+    weight_ref, grad_ref, code_ref, rad_ref, table_ref, pair_ref, cols_ref, grid_ref, own_ref, *refs
 ):
     bf16 = jnp.bfloat16
-    sent_refs, spread = refs[:-1], refs[-1]
-    rows = rows_ref[...]
+    sent_refs, (spread, filt_rows, sel_t, rad_twice) = refs[:-4], refs[-4:]
     block_len = own_ref.shape[1]
+
+    @pl.when(pl.program_id(0) == 0)
+    def _():
+        sel_t[...] = selector(code_ref).T.astype(bf16)
+        rad = masked_radial(code_ref, rad_ref)
+        rad_twice[...] = jnp.concatenate([rad, rad], axis=0).astype(bf16)
+        spread[:, G * GROUP :, :] = jnp.zeros(
+            (spread.shape[0], (G_PAD - G) * GROUP, LANES), jnp.float32
+        )
+
+    fill_filters(weight_ref, cols_ref, filt_rows)
     for tile in range(spread.shape[0]):
-        spread[tile] = (
+        spread[tile, : G * GROUP, :] = (
             grad_ref[:, :, tile * LANES : (tile + 1) * LANES]
             .astype(jnp.float32)
-            .reshape(spread.shape[1:])
+            .reshape(G * GROUP, LANES)
         )
 
     @pl.loop(0, GROUP // SUB)
     def _(batch):
         first = batch * SUB
         filters = [
-            split_parts(dot(rows, weight_ref[first + c], ((1,), (1,))), 1) for c in range(SUB)
+            filters_of(filt_rows, first + c).T[:SAMPLES_PAD].astype(bf16) for c in range(SUB)
         ]
-        filt_grid = dot(jnp.concatenate(filters, axis=0), rad_ref[...])
+        filt_grid = dot(jnp.concatenate(filters, axis=0), rad_twice[...])
         sides = []
+        for pair in range(0, SUB, 2):
+            grads = [
+                jnp.concatenate(
+                    [
+                        spread[tile, pl.ds(first + c, G_PAD, stride=GROUP), :].astype(bf16)
+                        for tile in range(spread.shape[0])
+                    ],
+                    axis=1,
+                )
+                for c in (pair, pair + 1)
+            ]
+            both = dot(pair_ref[...], jnp.concatenate(grads, axis=0))
+            for c in (pair, pair + 1):
+                weighted = both[(c - pair) * SAMPLES_PAD : (c - pair + 1) * SAMPLES_PAD]
+                grid_ref[first + c] = weighted.astype(bf16)
+                sides.append(
+                    (weighted * filt_grid[c * SAMPLES_PAD : (c + 1) * SAMPLES_PAD]).astype(bf16)
+                )
+        summed = dot(jnp.concatenate(sides, axis=0), sel_t[...]).astype(bf16)
+        placed = dot(
+            table_ref[...],
+            jnp.concatenate(
+                [summed[c * SAMPLES_PAD : (c + 1) * SAMPLES_PAD] for c in range(SUB)], axis=1
+            ),
+        ) * (1.0 / SAMPLES)
         for c in range(SUB):
-            grad = jnp.concatenate(
-                [
-                    spread[tile, pl.ds(first + c, G, stride=GROUP), :].astype(bf16)
-                    for tile in range(spread.shape[0])
-                ],
-                axis=1,
-            )
-            weighted = dot(rows, grad)
-            grid_ref[first + c] = weighted.astype(bf16)
-            sides.append(
-                (weighted * filt_grid[c * SAMPLES_PAD : (c + 1) * SAMPLES_PAD]).astype(bf16)
-            )
-        summed = dot(jnp.concatenate(sides, axis=0), sel_ref[...]).astype(bf16)
-        for c in range(SUB):
-            placed = dot(table_ref[...], summed[c * SAMPLES_PAD : (c + 1) * SAMPLES_PAD])
-            placed = (placed.T * (1.0 / SAMPLES))[:, :G]
+            turned = placed[:, c * LANES : (c + 1) * LANES].T[:, :G]
             blocks = [
-                placed[index * block_len : (index + 1) * block_len]
+                turned[index * block_len : (index + 1) * block_len]
                 for index in range(2 * REACH + 1)
             ]
             own_ref[first + c] = blocks.pop(REACH)
@@ -102,45 +142,58 @@
 
 
 def filter_kernel(
-    weight_ref, grid_ref, sel_ref, rad_ref, table_ref, rows_ref, rows_rest_ref, cols_ref, *refs
+    grid_ref, weight_ref, code_ref, rad_ref, table_t_ref, rows_ref, cols_ref, *refs
 ):
     bf16 = jnp.bfloat16
-    window_refs, (radial_ref, out_ref) = refs[:-2], refs[-2:]
+    window_refs, (radial_ref, out_ref, filt_rows, sel, rad_t) = refs[:-5], refs[-5:]
     basis_count = radial_ref.shape[0]
 
     @pl.when(pl.program_id(0) == 0)
     def _():
         radial_ref[...] = jnp.zeros_like(radial_ref)
+        sel[...] = selector(code_ref).astype(bf16)
+        rad_t[...] = masked_radial(code_ref, rad_ref).T.astype(bf16)
+
+    fill_filters(weight_ref, cols_ref, filt_rows)
+    block_len = window_refs[0].shape[1]
+    rest = jnp.zeros((LANES - len(window_refs) * block_len, G), bf16)
 
     @pl.loop(0, GROUP // SUB)
     def _(batch):
         first = batch * SUB
-        atom_grids = []
+        windows = []
         for c in range(SUB):
-            window = jnp.concatenate([ref[first + c] for ref in window_refs], axis=0)
-            atom_grids.append(
+            windows += [ref[first + c] for ref in window_refs] + [rest]
+        atom_grid = dot(rows_ref[...], jnp.concatenate(windows, axis=0), ((1,), (1,)))
+        atom_grid = (atom_grid[:SAMPLES_PAD] + atom_grid[SAMPLES_PAD:]).astype(bf16)
+        feat_grid = dot(
+            jnp.concatenate(
+                [atom_grid[:, c * LANES : (c + 1) * LANES] for c in range(SUB)], axis=0
+            ),
+            sel[...],
+        )
+        sides = jnp.concatenate(
+            [
                 (
-                    dot(rows_ref[...], window, ((1,), (1,)))
-                    + dot(rows_rest_ref[...], window, ((1,), (1,)))
+                    grid_ref[first + c].astype(jnp.float32)
+                    * feat_grid[c * SAMPLES_PAD : (c + 1) * SAMPLES_PAD]
                 ).astype(bf16)
-            )
-        feat_grid = dot(jnp.concatenate(atom_grids, axis=0), sel_ref[...])
-        sides = [
-            (
-                grid_ref[first + c].astype(jnp.float32)
-                * feat_grid[c * SAMPLES_PAD : (c + 1) * SAMPLES_PAD]
-            ).astype(bf16)
-            for c in range(SUB)
-        ]
-        summed = dot(jnp.concatenate(sides, axis=0), rad_ref[...]).astype(bf16)
-        radial_sum = radial_ref[...]
+                for c in range(SUB)
+            ],
+            axis=0,
+        )
+        summed = dot(sides, rad_t[...])
+        turned = jnp.concatenate(
+            [summed[c * SAMPLES_PAD : (c + 1) * SAMPLES_PAD].T for c in range(SUB)], axis=0
+        )
+        placed = dot(turned.astype(bf16), table_t_ref[...])
         for c in range(SUB):
-            filters = split_parts(dot(weight_ref[first + c], cols_ref[...]), 0)
-            parts = dot(filters, sides[c])
-            radial_sum = radial_sum + parts[:basis_count] + parts[basis_count:]
-            placed = dot(table_ref[...], summed[c * SAMPLES_PAD : (c + 1) * SAMPLES_PAD])
-            out_ref[first + c] = placed.T[:, :G]
-        radial_ref[...] = radial_sum
+            out_ref[first + c] = placed[c * basis_count : (c + 1) * basis_count, :G]
+        filters = jnp.concatenate(
+            [filters_of(filt_rows, first + c)[:, :SAMPLES_PAD] for c in range(SUB)], axis=1
+        )
+        parts = dot(filters.astype(bf16), sides)
+        radial_ref[...] += parts[:basis_count] + parts[basis_count:]
 
 
 def whole(x):
@@ -151,8 +204,9 @@
     return pl.BlockSpec((GROUP,) + tuple(shape), lambda i: (i, 0, 0))
 
 
-def grid_call(kernel, name, out_shape, out_specs, split, special, shared, split_last=(), scratch=()):
-    chan_count = split[0].shape[0]
+def grid_call(
+    kernel, name, chan_count, out_shape, out_specs, split, special, shared, split_last=(), scratch=()
+):
     return pl.pallas_call(
         kernel,
         grid=(chan_count // GROUP,),
@@ -292,9 +346,13 @@
 
 def local(feats, neighbors, counts, radial, filter_weight, message_grad):
     exact = basis_table()
-    table = jnp.asarray(exact, jnp.bfloat16)
-    rows_np = exact[:G].T.astype(jnp.bfloat16)
-    rows = jnp.asarray(rows_np)
+    rounded = exact.astype(jnp.bfloat16)
+    remainder = (exact - rounded.astype(np.float32)).astype(jnp.bfloat16)
+    table = jnp.asarray(rounded)
+    table_t = jnp.asarray(rounded.T)
+    pair_rows = jnp.asarray(np.kron(np.eye(2, dtype=np.float32), rounded.T.astype(np.float32)), jnp.bfloat16)
+    split_rows = jnp.asarray(np.concatenate([rounded[:G].T, remainder[:G].T], axis=0))
+    columns = jnp.asarray(np.pad(rounded[:G], ((0, 0), (0, -SAMPLES_PAD % LANES))))
     atom_count = lax.axis_size("atom")
     position = lax.axis_index("atom")
     block_len = feats.shape[3]
@@ -305,41 +363,45 @@
         own_block if offset == 0 else passed_along(own_block, "atom", -offset)
         for offset in offsets
     ]
-    window_len = len(offsets) * block_len
     sources = neighbors[0].reshape(-1)
     slot_index = (
         sources // block_len - position + REACH
     ) % atom_count * block_len + sources % block_len
     valid = (jnp.arange(SLOTS, dtype=jnp.int32)[None, :] < counts[0][:, None]).reshape(-1)
-    slots = jnp.arange(window_len, dtype=jnp.int32)
-    selector = ((slot_index[None, :] == slots[:, None]) & valid[None, :]).astype(jnp.bfloat16)
-    selector_rows = ((slot_index[:, None] == slots[None, :]) & valid[:, None]).astype(jnp.bfloat16)
-    radial_e = radial[0] * valid.astype(jnp.bfloat16)[None, :]
-    radial_twice = jnp.concatenate([radial_e, radial_e], axis=0)
-    rows_rest = jnp.asarray(exact[:G].T - np.asarray(rows_np, np.float32), jnp.bfloat16)
-    weight_c = jnp.transpose(filter_weight, (1, 0, 2))
-    weight_twice = jnp.concatenate([weight_c, weight_c], axis=1)
+    code = jnp.where(valid, slot_index, -1)[None, :]
+    radial_e = radial[0]
     basis_count = radial_e.shape[0]
     edges = radial_e.shape[1]
     block_shape = (chan_count, block_len, G)
+    weight_spec = pl.BlockSpec((basis_count, GROUP, G), lambda i: (0, i, 0))
+    filter_scratch = pltpu.VMEM(
+        (-(-SAMPLES_PAD // LANES), basis_count * GROUP, LANES), jnp.float32
+    )
     grid, own_grad, *outgoing = grid_call(
         feature_kernel,
         "feature_path",
+        chan_count,
         [
             jax.ShapeDtypeStruct((chan_count, SAMPLES_PAD, edges), jnp.bfloat16),
             jax.ShapeDtypeStruct(block_shape, jnp.float32),
         ]
         + [jax.ShapeDtypeStruct(block_shape, jnp.bfloat16)] * (2 * REACH),
         [grouped((SAMPLES_PAD, edges))] + [grouped(block_shape[1:])] * (2 * REACH + 1),
-        [weight_twice],
+        [],
         [
+            (filter_weight, weight_spec),
             (
                 jnp.transpose(message_grad[0], (1, 0, 2)),
                 pl.BlockSpec((G, GROUP, edges), lambda i: (0, i, 0)),
             )
         ],
-        [selector_rows, radial_twice, table, rows],
-        scratch=[pltpu.VMEM((edges // LANES, G * GROUP, LANES), jnp.float32)],
+        [code, radial_e, table, pair_rows, columns],
+        scratch=[
+            pltpu.VMEM((edges // LANES, G_PAD * GROUP, LANES), jnp.float32),
+            filter_scratch,
+            pltpu.VMEM((edges, LANES), jnp.bfloat16),
+            pltpu.VMEM((2 * basis_count, edges), jnp.bfloat16),
+        ],
     )
     arrived = [
         passed_along(block, "atom", offset)
@@ -348,6 +410,7 @@
     radial_local, weight_local = grid_call(
         filter_kernel,
         "filter_path",
+        chan_count,
         [
             jax.ShapeDtypeStruct((basis_count, edges), jnp.float32),
             jax.ShapeDtypeStruct((chan_count, basis_count, G), jnp.float32),
@@ -356,10 +419,15 @@
             pl.BlockSpec((basis_count, edges), lambda i: (0, 0)),
             grouped((basis_count, G)),
         ],
-        [weight_twice, grid],
-        [],
-        [selector, radial_e.T, table, rows, rows_rest, table[:G]],
+        [grid],
+        [(filter_weight, weight_spec)],
+        [code, radial_e, table_t, split_rows, columns],
         window,
+        scratch=[
+            filter_scratch,
+            pltpu.VMEM((LANES, edges), jnp.bfloat16),
+            pltpu.VMEM((edges, basis_count), jnp.bfloat16),
+        ],
     )
     sharers = atom_count * lax.axis_size("rep")
     weight_summed, radial_grad = sum_call(weight_local.reshape(sharers, -1, G), radial_local)

time: 99.2 us -> 84.4 us (0.85)
  Pallas kernels: 71.1 us -> 61.6 us
  other arithmetic: 5.55 us -> 2.32 us
  local copies, waits for them, and re-layouts: 6.5 us -> 4.59 us
    pallas_call x2, Pallas kernels: 53.7 us -> 44.1 us  [grid_call(): pl.pallas_call(kernel, grid=(chan_count // GROUP,), in_specs=[grouped(x.s...]
    unnamed x17 -> x15, local copies, waits for them, and re-layouts: 4.82 us -> 2.98 us
    convert_element_type x3 -> x0, other arithmetic: 1.53 us -> none  [the longest x1 0.86 us: local(): ((slot_index[:, None] == slots[None, :]) & valid[:, None]).astype(jnp.bfl...]
    concatenate x2 -> x0, other arithmetic: 1.38 us -> none  [the longest x1 0.76 us: local(): weight_twice = jnp.concatenate([weight_c, weight_c], axis=1)]
  transfers between devices with their start and end apart: 8 -> 8, of which waited for: 0 -> 0; matrix products, arithmetic and copies ran while one was open for 8% -> 4% of each run, Pallas kernels for 72% -> 73%
where the time goes in v4:
time: 84.4 us; the launch traced here: 84.1 us
  Pallas kernels  61.6 us (73%)
  starting transfers between devices  14.9 us (18%)
  local copies, waits for them, and re-layouts  4.59 us (5%)
  other arithmetic  2.32 us (3%)
    pallas_call x2, Pallas kernels, grid_call(): pl.pallas_call(kernel, grid=(chan_count // GROUP,), in_specs=[grouped(x.s...  44.1 us
    pallas_call x1, Pallas kernels, sum_call(): pl.pallas_call(sum_kernel, in_specs=[vmem, vmem], out_specs=[vmem, vmem],...  17.4 us
    ppermute x8, starting transfers between devices, passed_along(): return lax.ppermute(value, axis, pairs)  14.9 us
    unnamed x15, local copies, waits for them, and re-layouts  2.98 us
  transfers between devices with their start and end apart: 8, of which 0 were waited for; matrix products, arithmetic and copies ran while one was open for 4% of the time, Pallas kernels for 73%

profile of v4, /device:TPU:0, one launch (start us, length us, event | category | flops | bytes accessed | tf_op | source)
XLA Modules:
  0.0 84.1 jit_solution(4115659795250449662)
XLA Ops:
  0.6 3.1 %collective-permute-start.4 = (bf16[64,16,81]{2,1,0:T(8,128)(2,1)}, bf16[64,16,81]{2,1,0:T(8,128)(2,1)S(1)}, u32[]{:S(2)}, u32[]{:S(2)}) collective-permute-start(bf16[64,16,81]{2,1,0:T(8,128)(2,1)} %bitcast.24), channel_id=1, source_target_pairs={{0,8},{4,12},{8,16},{12,20},{16,24},{20,28},{24,0},{28,4},{1,9},{5... | collective-permute-start | bytes 497672 | tf_op jit(solution)/shard_map/ppermute | solution.py:42
  3.7 1.5 %collective-permute-start.5 = (bf16[64,16,81]{2,1,0:T(8,128)(2,1)}, bf16[64,16,81]{2,1,0:T(8,128)(2,1)S(1)}, u32[]{:S(2)}, u32[]{:S(2)}) collective-permute-start(bf16[64,16,81]{2,1,0:T(8,128)(2,1)} %bitcast.25), channel_id=1, source_target_pairs={{0,4},{4,8},{8,12},{12,16},{16,20},{20,24},{24,28},{28,0},{1,5},{5... | collective-permute-start | bytes 497672 | tf_op jit(solution)/shard_map/ppermute | solution.py:42
  5.2 3.2 %collective-permute-start.6 = (bf16[64,16,81]{2,1,0:T(8,128)(2,1)}, bf16[64,16,81]{2,1,0:T(8,128)(2,1)S(1)}, u32[]{:S(2)}, u32[]{:S(2)}) collective-permute-start(bf16[64,16,81]{2,1,0:T(8,128)(2,1)} %bitcast.26), channel_id=1, source_target_pairs={{0,28},{4,0},{8,4},{12,8},{16,12},{20,16},{24,20},{28,24},{1,29},{... | collective-permute-start | bytes 497672 | tf_op jit(solution)/shard_map/ppermute | solution.py:42
  8.4 0.3 collective-permute-start.7
  8.7 0.7 iota_compare_fusion
  9.5 0.1 lt.40
  9.5 0.8 reshape_squeeze.3
  10.3 0.6 fusion.1.code_ref
  10.9 23.4 %feature_path.1 = (bf16[64,176,512]{2,1,0:T(8,128)(2,1)}, f32[64,16,81]{2,1,0:T(8,128)}, bf16[64,16,81]{2,1,0:T(8,128)(2,1)}, bf16[64,16,81]{2,1,0:T(8,128)(2,1)...) custom-call(bf16[8,64,81]{2,1,0:T(8,128)(2,1)} %weight_ref.3, bf16[81,64,512]{2,1,0:T(8,128)(2,1)} %bitcast.23, ...), custom_call_target="tpu_custom_call" | custom-call | flops 10240000000 | bytes 16000000 | tf_op jit(solution)/shard_map/feature_path/pallas_call | solution.py:210
  34.3 1.8 %collective-permute-start.3 = (bf16[64,16,81]{2,1,0:T(8,128)(2,1)}, bf16[64,16,81]{2,1,0:T(8,128)(2,1)S(1)}, u32[]{:S(2)}, u32[]{:S(2)}) collective-permute-start(bf16[64,16,81]{2,1,0:T(8,128)(2,1)} %get-tuple-element.17), channel_id=1, source_target_pairs={{0,8},{4,12},{8,16},{12,20},{16,24},{20,28},{24,0},{28,4},{1,9},{5... | collective-permute-start | bytes 497672 | tf_op jit(solution)/shard_map/ppermute | solution.py:42
  36.1 0.0 collective-permute-done.5.refs_1_
  36.1 4.7 %collective-permute-start.1 = (bf16[64,16,81]{2,1,0:T(8,128)(2,1)}, bf16[64,16,81]{2,1,0:T(8,128)(2,1)S(1)}, u32[]{:S(2)}, u32[]{:S(2)}) collective-permute-start(bf16[64,16,81]{2,1,0:T(8,128)(2,1)} %get-tuple-element.15), channel_id=1, source_target_pairs={{0,28},{4,0},{8,4},{12,8},{16,12},{20,16},{24,20},{28,24},{1,29},{... | collective-permute-start | bytes 497672 | tf_op jit(solution)/shard_map/ppermute | solution.py:42
  40.8 0.3 collective-permute-start
  41.1 0.4 copy-done.5
  41.6 0.3 copy-done.6
  41.8 20.8 %filter_path.1 = (f32[8,512]{1,0:T(8,128)}, f32[64,8,81]{2,1,0:T(8,128)}) custom-call(bf16[64,176,512]{2,1,0:T(8,128)(2,1)} %get-tuple-element.18.grid_ref, bf16[8,64,81]{2,1,0:T(8,128)(2,1)} %weight_ref.3, s32[1,512]{1,0:T(1,128)} %fusion.1.code_ref, bf16[8,512]{1,0:T(8,128)(2,1)} %bitcast.30, bf16[176,96]{1,0:T(8,128)(2,1)} %constant.62.clone.table_t_ref, ...), custom_call_target="tpu_custom_call" | custom-call | flops 10240000000 | bytes 16000000 | tf_op jit(solution)/shard_map/filter_path/pallas_call | solution.py:210
  62.6 0.9 %copy-done = f32[64,8,81]{2,1,0:T(8,128)S(1)} copy-done((f32[64,8,81]{2,1,0:T(8,128)S(1)}, f32[64,8,81]{2,1,0:T(8,128)}, u32[]{:S(2)}) %copy-start) | copy-done | bytes 165912
  63.6 0.7 copy-done.1
  64.3 17.4 %sums.1 = (f32[16,32,81]{2,1,0:T(8,128)S(1)}, f32[8,512]{1,0:T(8,128)S(1)}) custom-call(f32[16,32,81]{2,1,0:T(8,128)S(1)} %bitcast.18, f32[8,512]{1,0:T(8,128)S(1)} %copy-done.1), custom_call_target="tpu_custom_call" | custom-call | tf_op jit(solution)/shard_map/sums/pallas_call | solution.py:327
  81.8 0.8 copy.16
  82.5 0.0 collective-permute-done.3
  82.5 0.0 collective-permute-done.2
  82.6 0.9 %add_bitcast_fusion = f32[1,64,81,16]{2,3,1,0:T(8,128)} fusion(bf16[64,16,81]{2,1,0:T(8,128)(2,1)S(1)} %collective-permute-done.3, bf16[64,16,81]{2,1,0:T(8,128)(2,1)S(1)} %collective-permute-done.2, bf16[64,16,81]{2,1,0:T(8,128)(2,1)S(1)} %collective-permute-done.1, f32[64,16,81]{2,1,0:T(8,128)S(1)} %copy-done.2, bf16[64,16,81]{2,1,0:T(8,128)(2,1)S(1)} %collective-permute-done), kind=kLoop, calls=%fused_computation | loop fusion | flops 663552 | bytes 1327104 | tf_op jit(solution)/shard_map/broadcast_in_dim | solution.py:439
  83.5 0.6 copy.18
  (17 shorter events, 0.1 us)
Async XLA Ops:
  0.6 35.5 %collective-permute-start.4 = (bf16[64,16,81]{2,1,0:T(8,128)(2,1)}, bf16[64,16,81]{2,1,0:T(8,128)(2,1)S(1)}, u32[]{:S(2)}, u32[]{:S(2)}) collective-permute-start(bf16[64,16,81]{2,1,0:T(8,128)(2,1)} %bitcast.24), channel_id=1, source_target_pairs={{0,8},{4,12},{8,16},{12,20},{16,24},{20,28},{24,0},{28,4},{1,9},{5... | collective-permute-start | bytes 497672 | tf_op jit(solution)/shard_map/ppermute | solution.py:42
  3.7 32.4 %collective-permute-start.5 = (bf16[64,16,81]{2,1,0:T(8,128)(2,1)}, bf16[64,16,81]{2,1,0:T(8,128)(2,1)S(1)}, u32[]{:S(2)}, u32[]{:S(2)}) collective-permute-start(bf16[64,16,81]{2,1,0:T(8,128)(2,1)} %bitcast.25), channel_id=1, source_target_pairs={{0,4},{4,8},{8,12},{12,16},{16,20},{20,24},{24,28},{28,0},{1,5},{5... | collective-permute-start | bytes 497672 | tf_op jit(solution)/shard_map/ppermute | solution.py:42
  5.2 35.6 %collective-permute-start.6 = (bf16[64,16,81]{2,1,0:T(8,128)(2,1)}, bf16[64,16,81]{2,1,0:T(8,128)(2,1)S(1)}, u32[]{:S(2)}, u32[]{:S(2)}) collective-permute-start(bf16[64,16,81]{2,1,0:T(8,128)(2,1)} %bitcast.26), channel_id=1, source_target_pairs={{0,28},{4,0},{8,4},{12,8},{16,12},{20,16},{24,20},{28,24},{1,29},{... | collective-permute-start | bytes 497672 | tf_op jit(solution)/shard_map/ppermute | solution.py:42
  8.4 32.7 %collective-permute-start.7 = (bf16[64,16,81]{2,1,0:T(8,128)(2,1)}, bf16[64,16,81]{2,1,0:T(8,128)(2,1)S(1)}, u32[]{:S(2)}, u32[]{:S(2)}) collective-permute-start(bf16[64,16,81]{2,1,0:T(8,128)(2,1)} %bitcast.27), channel_id=1, source_target_pairs={{0,24},{4,28},{8,0},{12,4},{16,8},{20,12},{24,16},{28,20},{1,25},{... | collective-permute-start | bytes 497672 | tf_op jit(solution)/shard_map/ppermute | solution.py:42
  34.3 48.2 %collective-permute-start.3 = (bf16[64,16,81]{2,1,0:T(8,128)(2,1)}, bf16[64,16,81]{2,1,0:T(8,128)(2,1)S(1)}, u32[]{:S(2)}, u32[]{:S(2)}) collective-permute-start(bf16[64,16,81]{2,1,0:T(8,128)(2,1)} %get-tuple-element.17), channel_id=1, source_target_pairs={{0,8},{4,12},{8,16},{12,20},{16,24},{20,28},{24,0},{28,4},{1,9},{5... | collective-permute-start | bytes 497672 | tf_op jit(solution)/shard_map/ppermute | solution.py:42
  36.1 5.0 %copy-start.3 = (bf16[64,16,81]{2,1,0:T(8,128)(2,1)}, bf16[64,16,81]{2,1,0:T(8,128)(2,1)S(1)}, u32[]{:S(2)}) copy-start(bf16[64,16,81]{2,1,0:T(8,128)(2,1)S(1)} %collective-permute-done.4.refs_0_) | copy-start | bytes 497668
  36.1 46.4 %collective-permute-start.2 = (bf16[64,16,81]{2,1,0:T(8,128)(2,1)}, bf16[64,16,81]{2,1,0:T(8,128)(2,1)S(1)}, u32[]{:S(2)}, u32[]{:S(2)}) collective-permute-start(bf16[64,16,81]{2,1,0:T(8,128)(2,1)} %get-tuple-element.16), channel_id=1, source_target_pairs={{0,4},{4,8},{8,12},{12,16},{16,20},{20,24},{24,28},{28,0},{1,5},{5... | collective-permute-start | bytes 497672 | tf_op jit(solution)/shard_map/ppermute | solution.py:42
  36.1 5.0 %copy-start.4 = (bf16[64,16,81]{2,1,0:T(8,128)(2,1)}, bf16[64,16,81]{2,1,0:T(8,128)(2,1)S(1)}, u32[]{:S(2)}) copy-start(bf16[64,16,81]{2,1,0:T(8,128)(2,1)S(1)} %collective-permute-done.5.refs_1_) | copy-start | bytes 497668
  36.1 46.4 %collective-permute-start.1 = (bf16[64,16,81]{2,1,0:T(8,128)(2,1)}, bf16[64,16,81]{2,1,0:T(8,128)(2,1)S(1)}, u32[]{:S(2)}, u32[]{:S(2)}) collective-permute-start(bf16[64,16,81]{2,1,0:T(8,128)(2,1)} %get-tuple-element.15), channel_id=1, source_target_pairs={{0,28},{4,0},{8,4},{12,8},{16,12},{20,16},{24,20},{28,24},{1,29},{... | collective-permute-start | bytes 497672 | tf_op jit(solution)/shard_map/ppermute | solution.py:42
  40.8 0.7 copy-start.5
  40.8 41.7 %collective-permute-start = (bf16[64,16,81]{2,1,0:T(8,128)(2,1)}, bf16[64,16,81]{2,1,0:T(8,128)(2,1)S(1)}, u32[]{:S(2)}, u32[]{:S(2)}) collective-permute-start(bf16[64,16,81]{2,1,0:T(8,128)(2,1)} %get-tuple-element.14), channel_id=1, source_target_pairs={{0,24},{4,28},{8,0},{12,4},{16,8},{20,12},{24,16},{28,20},{1,25},{... | collective-permute-start | bytes 497672 | tf_op jit(solution)/shard_map/ppermute | solution.py:42
  41.1 0.7 copy-start.6
  41.8 40.7 %copy-start.2 = (f32[64,16,81]{2,1,0:T(8,128)S(1)}, f32[64,16,81]{2,1,0:T(8,128)}, u32[]{:S(2)}) copy-start(f32[64,16,81]{2,1,0:T(8,128)} %get-tuple-element.13) | copy-start | bytes 995332
  62.6 0.9 %copy-start = (f32[64,8,81]{2,1,0:T(8,128)S(1)}, f32[64,8,81]{2,1,0:T(8,128)}, u32[]{:S(2)}) copy-start(f32[64,8,81]{2,1,0:T(8,128)} %get-tuple-element.19) | copy-start | bytes 497668
  63.6 0.7 copy-start.1

commit v5 on v4

--- a/solution.py
+++ b/solution.py
@@ -17,7 +17,7 @@
 G = 81
 G_PAD = 96
 GROUP = 16
-SUB = 4
+SUB = 8
 LANES = 128
 
 
@@ -187,8 +187,8 @@
             [summed[c * SAMPLES_PAD : (c + 1) * SAMPLES_PAD].T for c in range(SUB)], axis=0
         )
         placed = dot(turned.astype(bf16), table_t_ref[...])
-        for c in range(SUB):
-            out_ref[first + c] = placed[c * basis_count : (c + 1) * basis_count, :G]
+        span = SUB * basis_count
+        out_ref[pl.ds(pl.multiple_of(batch * span, span), span), :] = placed[:, :G].astype(bf16)
         filters = jnp.concatenate(
             [filters_of(filt_rows, first + c)[:, :SAMPLES_PAD] for c in range(SUB)], axis=1
         )
@@ -226,7 +226,7 @@
 
 
 def sum_kernel(
-    weight_ref, radial_ref, weight_out, radial_out, parts, slots, send1, recv1, send2, recv2, send3, recv3
+    weight_ref, radial_ref, weight_out, radial_out, parts, slots, send1, recv1, send2, recv2, send3, recv3, own
 ):
     atoms, reps, chans = (lax.axis_size(name) for name in ("atom", "rep", "chan"))
     atom, rep, chan = (lax.axis_index(name) for name in ("atom", "rep", "chan"))
@@ -240,6 +240,10 @@
     def other(step):
         return {"atom": atom, "chan": lax.rem(chan + step, chans), "rep": rep}
 
+    own_chunk = pltpu.make_async_copy(weight_ref.at[me], parts.at[0], own.at[0])
+    own_radial = pltpu.make_async_copy(radial_ref, slots.at[chan], own.at[1])
+    own_chunk.start()
+    own_radial.start()
     barrier = pltpu.get_barrier_semaphore()
 
     @pl.loop(1, count)
@@ -291,16 +295,16 @@
 
     for step in range(1, chans):
         radial_copy(step).start()
-    slots[chan] = radial_ref[...]
 
     @pl.loop(1, count)
     def _(step):
         chunk_copy(step).wait_recv()
 
-    total = weight_ref[me]
+    own_chunk.wait()
+    total = parts[0].astype(jnp.float32)
     for step in range(1, count):
-        total = total + parts[step]
-    weight_out[me] = total
+        total = total + parts[step].astype(jnp.float32)
+    weight_out[me] = total.astype(weight_out.dtype)
 
     @pl.loop(1, count)
     def _(step):
@@ -308,6 +312,7 @@
 
     for step in range(1, chans):
         radial_copy(step).wait()
+    own_radial.wait()
     radial_total = slots[0]
     for index in range(1, chans):
         radial_total = radial_total + slots[index]
@@ -323,23 +328,23 @@
     chans = lax.axis_size("chan")
     count = weight.shape[0]
     vmem = pl.BlockSpec(memory_space=pltpu.VMEM)
-    sems = [pltpu.SemaphoreType.DMA((size,)) for size in (count, count, chans, chans, count, count)]
+    anywhere = pl.BlockSpec(memory_space=pl.ANY)
+    sizes = (count, count, chans, chans, count, count, 2)
+    sems = [pltpu.SemaphoreType.DMA((size,)) for size in sizes]
     return pl.pallas_call(
         sum_kernel,
-        in_specs=[vmem, vmem],
+        in_specs=[anywhere, anywhere],
         out_specs=[vmem, vmem],
         out_shape=[
-            jax.ShapeDtypeStruct(weight.shape, jnp.float32),
+            jax.ShapeDtypeStruct(weight.shape, weight.dtype),
             jax.ShapeDtypeStruct(radial.shape, jnp.float32),
         ],
         scratch_shapes=[
-            pltpu.VMEM(weight.shape, jnp.float32),
+            pltpu.VMEM(weight.shape, weight.dtype),
             pltpu.VMEM((chans,) + radial.shape, jnp.float32),
         ]
         + sems,
-        compiler_params=pltpu.CompilerParams(
-            collective_id=0, has_side_effects=True, vmem_limit_bytes=16 * 1024 * 1024
-        ),
+        compiler_params=pltpu.CompilerParams(collective_id=0, has_side_effects=True),
         name="sums",
     )(weight, radial)
 
@@ -413,11 +418,11 @@
         chan_count,
         [
             jax.ShapeDtypeStruct((basis_count, edges), jnp.float32),
-            jax.ShapeDtypeStruct((chan_count, basis_count, G), jnp.float32),
+            jax.ShapeDtypeStruct((chan_count * basis_count, G), jnp.bfloat16),
         ],
         [
             pl.BlockSpec((basis_count, edges), lambda i: (0, 0)),
-            grouped((basis_count, G)),
+            pl.BlockSpec((GROUP * basis_count, G), lambda i: (i, 0)),
         ],
         [grid],
         [(filter_weight, weight_spec)],
@@ -432,7 +437,7 @@
     sharers = atom_count * lax.axis_size("rep")
     weight_summed, radial_grad = sum_call(weight_local.reshape(sharers, -1, G), radial_local)
     weight_summed = jnp.transpose(weight_summed.reshape(chan_count, basis_count, G), (1, 0, 2))
-    weight_grad = weight_summed * (1.0 / (SAMPLES * sharers * block_len))
+    weight_grad = weight_summed.astype(jnp.float32) * (1.0 / (SAMPLES * sharers * block_len))
     returned_sum = own_grad
     for block in arrived:
         returned_sum = returned_sum + block.astype(jnp.float32)

time: 84.4 us -> 75.2 us (0.89)
  Pallas kernels: 61.6 us -> 52.5 us
  local copies, waits for them, and re-layouts: 4.59 us -> 3.65 us
    pallas_call x2, Pallas kernels: 44.1 us -> 37.8 us  [grid_call(): pl.pallas_call(kernel, grid=(chan_count // GROUP,), in_specs=[grouped(x.s...]
    pallas_call x1, Pallas kernels: 17.4 us -> 14.7 us  [sum_call(): pl.pallas_call(sum_kernel, in_specs=[anywhere, anywhere], out_specs=[vmem...]
    unnamed x15 -> x11, local copies, waits for them, and re-layouts: 2.98 us -> 2.03 us
    mul x1, other arithmetic: 0.03 us -> 0.93 us  [local(): weight_summed.astype(jnp.float32) * (1.0 / (SAMPLES * sharers * block_len))]
  transfers between devices with their start and end apart: 8 -> 8, of which waited for: 0 -> 0; matrix products, arithmetic and copies ran while one was open for 4% -> 5% of each run, Pallas kernels for 73% -> 70%
where the time goes in v5:
time: 75.2 us; the launch traced here: 74.9 us
  Pallas kernels  52.5 us (70%)
  starting transfers between devices  14.9 us (20%)
  local copies, waits for them, and re-layouts  3.65 us (5%)
  other arithmetic  3.16 us (4%)
    pallas_call x2, Pallas kernels, grid_call(): pl.pallas_call(kernel, grid=(chan_count // GROUP,), in_specs=[grouped(x.s...  37.8 us
    ppermute x8, starting transfers between devices, passed_along(): return lax.ppermute(value, axis, pairs)  14.9 us
    pallas_call x1, Pallas kernels, sum_call(): pl.pallas_call(sum_kernel, in_specs=[anywhere, anywhere], out_specs=[vmem...  14.7 us
    unnamed x11, local copies, waits for them, and re-layouts  2.03 us
  transfers between devices with their start and end apart: 8, of which 0 were waited for; matrix products, arithmetic and copies ran while one was open for 5% of the time, Pallas kernels for 70%

profile of v5, /device:TPU:0, one launch (start us, length us, event | category | flops | bytes accessed | tf_op | source)
XLA Modules:
  0.0 74.9 jit_solution(4396470823102713847)
XLA Ops:
  0.6 3.1 %collective-permute-start.4 = (bf16[64,16,81]{2,1,0:T(8,128)(2,1)}, bf16[64,16,81]{2,1,0:T(8,128)(2,1)S(1)}, u32[]{:S(2)}, u32[]{:S(2)}) collective-permute-start(bf16[64,16,81]{2,1,0:T(8,128)(2,1)} %bitcast.24), channel_id=1, source_target_pairs={{0,8},{4,12},{8,16},{12,20},{16,24},{20,28},{24,0},{28,4},{1,9},{5... | collective-permute-start | bytes 497672 | tf_op jit(solution)/shard_map/ppermute | solution.py:42
  3.7 1.5 %collective-permute-start.5 = (bf16[64,16,81]{2,1,0:T(8,128)(2,1)}, bf16[64,16,81]{2,1,0:T(8,128)(2,1)S(1)}, u32[]{:S(2)}, u32[]{:S(2)}) collective-permute-start(bf16[64,16,81]{2,1,0:T(8,128)(2,1)} %bitcast.25), channel_id=1, source_target_pairs={{0,4},{4,8},{8,12},{12,16},{16,20},{20,24},{24,28},{28,0},{1,5},{5... | collective-permute-start | bytes 497672 | tf_op jit(solution)/shard_map/ppermute | solution.py:42
  5.2 3.2 %collective-permute-start.6 = (bf16[64,16,81]{2,1,0:T(8,128)(2,1)}, bf16[64,16,81]{2,1,0:T(8,128)(2,1)S(1)}, u32[]{:S(2)}, u32[]{:S(2)}) collective-permute-start(bf16[64,16,81]{2,1,0:T(8,128)(2,1)} %bitcast.26), channel_id=1, source_target_pairs={{0,28},{4,0},{8,4},{12,8},{16,12},{20,16},{24,20},{28,24},{1,29},{... | collective-permute-start | bytes 497672 | tf_op jit(solution)/shard_map/ppermute | solution.py:42
  8.4 0.3 collective-permute-start.7
  8.7 0.7 iota_compare_fusion
  9.5 0.1 lt.40
  9.5 0.8 %reshape_squeeze.3 = s32[1,512]{1,0:T(1,128)S(1)} reshape(s32[1,16,32]{2,1,0:T(8,128)} %param.12) | data formatting | bytes 4096 | tf_op jit(solution)/shard_map/reshape;squeeze | solution.py:371
  10.3 0.6 fusion.1.code_ref
  10.9 19.6 %feature_path.1 = (bf16[64,176,512]{2,1,0:T(8,128)(2,1)}, f32[64,16,81]{2,1,0:T(8,128)}, bf16[64,16,81]{2,1,0:T(8,128)(2,1)}, bf16[64,16,81]{2,1,0:T(8,128)(2,1)...) custom-call(bf16[8,64,81]{2,1,0:T(8,128)(2,1)} %weight_ref.3, bf16[81,64,512]{2,1,0:T(8,128)(2,1)} %bitcast.23, ...), custom_call_target="tpu_custom_call" | custom-call | flops 10240000000 | bytes 16000000 | tf_op jit(solution)/shard_map/feature_path/pallas_call | solution.py:210
  30.5 1.8 %collective-permute-start.3 = (bf16[64,16,81]{2,1,0:T(8,128)(2,1)}, bf16[64,16,81]{2,1,0:T(8,128)(2,1)S(1)}, u32[]{:S(2)}, u32[]{:S(2)}) collective-permute-start(bf16[64,16,81]{2,1,0:T(8,128)(2,1)} %get-tuple-element.17), channel_id=1, source_target_pairs={{0,8},{4,12},{8,16},{12,20},{16,24},{20,28},{24,0},{28,4},{1,9},{5... | collective-permute-start | bytes 497672 | tf_op jit(solution)/shard_map/ppermute | solution.py:42
  32.3 0.0 collective-permute-done.5.refs_1_
  32.3 4.7 %collective-permute-start.1 = (bf16[64,16,81]{2,1,0:T(8,128)(2,1)}, bf16[64,16,81]{2,1,0:T(8,128)(2,1)S(1)}, u32[]{:S(2)}, u32[]{:S(2)}) collective-permute-start(bf16[64,16,81]{2,1,0:T(8,128)(2,1)} %get-tuple-element.15), channel_id=1, source_target_pairs={{0,28},{4,0},{8,4},{12,8},{16,12},{20,16},{24,20},{28,24},{1,29},{... | collective-permute-start | bytes 497672 | tf_op jit(solution)/shard_map/ppermute | solution.py:42
  37.0 0.3 collective-permute-start
  37.3 0.0 collective-permute-done.7.refs_4_
  37.4 0.4 copy-done.3
  37.7 0.3 copy-done.4
  38.0 18.1 %filter_path.1 = (f32[8,512]{1,0:T(8,128)}, bf16[512,81]{1,0:T(8,128)(2,1)}) custom-call(bf16[64,176,512]{2,1,0:T(8,128)(2,1)} %get-tuple-element.18.grid_ref, bf16[8,64,81]{2,1,0:T(8,128)(2,1)} %weight_ref.3, s32[1,512]{1,0:T(1,128)} %fusion.1.code_ref, bf16[8,512]{1,0:T(8,128)(2,1)} %bitcast.30, bf16[176,96]{1,0:T(8,128)(2,1)} %constant.62.clone.table_t_ref, ...), custom_call_target="tpu_custom_call" | custom-call | flops 10240000000 | bytes 16000000 | tf_op jit(solution)/shard_map/filter_path/pallas_call | solution.py:210
  56.2 14.7 %sums.1 = (bf16[16,32,81]{2,1,0:T(8,128)(2,1)}, f32[8,512]{1,0:T(8,128)}) custom-call(bf16[16,32,81]{2,1,0:T(8,128)(2,1)} %bitcast.20, f32[8,512]{1,0:T(8,128)} %get-tuple-element.20.radial_ref), custom_call_target="tpu_custom_call" | custom-call | tf_op jit(solution)/shard_map/sums/pallas_call | solution.py:334
  70.9 0.9 %convert_multiply_fusion = f32[16,32,81]{2,1,0:T(8,128)S(1)} fusion(bf16[16,32,81]{2,1,0:T(8,128)(2,1)} %get-tuple-element.22), kind=kLoop, calls=%fused_computation.2 | loop fusion | flops 82944 | bytes 248832 | tf_op jit(solution)/shard_map/mul | solution.py:440
  71.9 0.8 %copy.16 = f32[64,8,81]{2,0,1:T(8,128)} copy(f32[64,8,81]{2,1,0:T(8,128)S(1)} %bitcast.18) | data formatting | bytes 331776 | tf_op jit(solution)/shard_map/mul | solution.py:440
  72.6 0.0 collective-permute-done.1
  72.6 0.0 collective-permute-done
  72.6 0.9 %add_bitcast_fusion = f32[1,64,81,16]{2,3,1,0:T(8,128)} fusion(bf16[64,16,81]{2,1,0:T(8,128)(2,1)S(1)} %collective-permute-done.3, bf16[64,16,81]{2,1,0:T(8,128)(2,1)S(1)} %collective-permute-done.2, bf16[64,16,81]{2,1,0:T(8,128)(2,1)S(1)} %collective-permute-done.1, f32[64,16,81]{2,1,0:T(8,128)S(1)} %copy-done, bf16[64,16,81]{2,1,0:T(8,128)(2,1)S(1)} %collective-permute-done), kind=kLoop, calls=%fused_computation | loop fusion | flops 663552 | bytes 1327104 | tf_op jit(solution)/shard_map/broadcast_in_dim | solution.py:444
  73.6 1.3 %copy.18 = f32[1,8,512]{2,1,0:T(8,128)} copy(f32[1,8,512]{2,1,0:T(8,128)} %bitcast.21) | data formatting | bytes 32768
  (13 shorter events, 0.0 us)
Async XLA Ops:
  0.6 31.7 %collective-permute-start.4 = (bf16[64,16,81]{2,1,0:T(8,128)(2,1)}, bf16[64,16,81]{2,1,0:T(8,128)(2,1)S(1)}, u32[]{:S(2)}, u32[]{:S(2)}) collective-permute-start(bf16[64,16,81]{2,1,0:T(8,128)(2,1)} %bitcast.24), channel_id=1, source_target_pairs={{0,8},{4,12},{8,16},{12,20},{16,24},{20,28},{24,0},{28,4},{1,9},{5... | collective-permute-start | bytes 497672 | tf_op jit(solution)/shard_map/ppermute | solution.py:42
  3.7 28.6 %collective-permute-start.5 = (bf16[64,16,81]{2,1,0:T(8,128)(2,1)}, bf16[64,16,81]{2,1,0:T(8,128)(2,1)S(1)}, u32[]{:S(2)}, u32[]{:S(2)}) collective-permute-start(bf16[64,16,81]{2,1,0:T(8,128)(2,1)} %bitcast.25), channel_id=1, source_target_pairs={{0,4},{4,8},{8,12},{12,16},{16,20},{20,24},{24,28},{28,0},{1,5},{5... | collective-permute-start | bytes 497672 | tf_op jit(solution)/shard_map/ppermute | solution.py:42
  5.2 31.8 %collective-permute-start.6 = (bf16[64,16,81]{2,1,0:T(8,128)(2,1)}, bf16[64,16,81]{2,1,0:T(8,128)(2,1)S(1)}, u32[]{:S(2)}, u32[]{:S(2)}) collective-permute-start(bf16[64,16,81]{2,1,0:T(8,128)(2,1)} %bitcast.26), channel_id=1, source_target_pairs={{0,28},{4,0},{8,4},{12,8},{16,12},{20,16},{24,20},{28,24},{1,29},{... | collective-permute-start | bytes 497672 | tf_op jit(solution)/shard_map/ppermute | solution.py:42
  8.4 28.9 %collective-permute-start.7 = (bf16[64,16,81]{2,1,0:T(8,128)(2,1)}, bf16[64,16,81]{2,1,0:T(8,128)(2,1)S(1)}, u32[]{:S(2)}, u32[]{:S(2)}) collective-permute-start(bf16[64,16,81]{2,1,0:T(8,128)(2,1)} %bitcast.27), channel_id=1, source_target_pairs={{0,24},{4,28},{8,0},{12,4},{16,8},{20,12},{24,16},{28,20},{1,25},{... | collective-permute-start | bytes 497672 | tf_op jit(solution)/shard_map/ppermute | solution.py:42
  30.5 42.1 %collective-permute-start.3 = (bf16[64,16,81]{2,1,0:T(8,128)(2,1)}, bf16[64,16,81]{2,1,0:T(8,128)(2,1)S(1)}, u32[]{:S(2)}, u32[]{:S(2)}) collective-permute-start(bf16[64,16,81]{2,1,0:T(8,128)(2,1)} %get-tuple-element.17), channel_id=1, source_target_pairs={{0,8},{4,12},{8,16},{12,20},{16,24},{20,28},{24,0},{28,4},{1,9},{5... | collective-permute-start | bytes 497672 | tf_op jit(solution)/shard_map/ppermute | solution.py:42
  32.3 5.1 %copy-start.1 = (bf16[64,16,81]{2,1,0:T(8,128)(2,1)}, bf16[64,16,81]{2,1,0:T(8,128)(2,1)S(1)}, u32[]{:S(2)}) copy-start(bf16[64,16,81]{2,1,0:T(8,128)(2,1)S(1)} %collective-permute-done.4.refs_0_) | copy-start | bytes 497668
  32.3 40.3 %collective-permute-start.2 = (bf16[64,16,81]{2,1,0:T(8,128)(2,1)}, bf16[64,16,81]{2,1,0:T(8,128)(2,1)S(1)}, u32[]{:S(2)}, u32[]{:S(2)}) collective-permute-start(bf16[64,16,81]{2,1,0:T(8,128)(2,1)} %get-tuple-element.16), channel_id=1, source_target_pairs={{0,4},{4,8},{8,12},{12,16},{16,20},{20,24},{24,28},{28,0},{1,5},{5... | collective-permute-start | bytes 497672 | tf_op jit(solution)/shard_map/ppermute | solution.py:42
  32.3 5.0 %copy-start.2 = (bf16[64,16,81]{2,1,0:T(8,128)(2,1)}, bf16[64,16,81]{2,1,0:T(8,128)(2,1)S(1)}, u32[]{:S(2)}) copy-start(bf16[64,16,81]{2,1,0:T(8,128)(2,1)S(1)} %collective-permute-done.5.refs_1_) | copy-start | bytes 497668
  32.3 40.3 %collective-permute-start.1 = (bf16[64,16,81]{2,1,0:T(8,128)(2,1)}, bf16[64,16,81]{2,1,0:T(8,128)(2,1)S(1)}, u32[]{:S(2)}, u32[]{:S(2)}) collective-permute-start(bf16[64,16,81]{2,1,0:T(8,128)(2,1)} %get-tuple-element.15), channel_id=1, source_target_pairs={{0,28},{4,0},{8,4},{12,8},{16,12},{20,16},{24,20},{28,24},{1,29},{... | collective-permute-start | bytes 497672 | tf_op jit(solution)/shard_map/ppermute | solution.py:42
  37.0 0.7 copy-start.3
  37.0 35.6 %collective-permute-start = (bf16[64,16,81]{2,1,0:T(8,128)(2,1)}, bf16[64,16,81]{2,1,0:T(8,128)(2,1)S(1)}, u32[]{:S(2)}, u32[]{:S(2)}) collective-permute-start(bf16[64,16,81]{2,1,0:T(8,128)(2,1)} %get-tuple-element.14), channel_id=1, source_target_pairs={{0,24},{4,28},{8,0},{12,4},{16,8},{20,12},{24,16},{28,20},{1,25},{... | collective-permute-start | bytes 497672 | tf_op jit(solution)/shard_map/ppermute | solution.py:42
  37.3 0.7 copy-start.4
  38.0 34.6 %copy-start = (f32[64,16,81]{2,1,0:T(8,128)S(1)}, f32[64,16,81]{2,1,0:T(8,128)}, u32[]{:S(2)}) copy-start(f32[64,16,81]{2,1,0:T(8,128)} %get-tuple-element.13) | copy-start | bytes 995332

commit v6 on v5

--- a/solution.py
+++ b/solution.py
@@ -17,7 +17,7 @@
 G = 81
 G_PAD = 96
 GROUP = 16
-SUB = 8
+SUB = 16
 LANES = 128
 
 
@@ -186,8 +186,11 @@
         turned = jnp.concatenate(
             [summed[c * SAMPLES_PAD : (c + 1) * SAMPLES_PAD].T for c in range(SUB)], axis=0
         )
-        placed = dot(turned.astype(bf16), table_t_ref[...])
+        coarse = turned.astype(bf16)
+        fine = (turned - coarse.astype(jnp.float32)).astype(bf16)
         span = SUB * basis_count
+        placed = dot(jnp.concatenate([coarse, fine], axis=0), table_t_ref[0])
+        placed = placed[:span] + placed[span:] + dot(coarse, table_t_ref[1])
         out_ref[pl.ds(pl.multiple_of(batch * span, span), span), :] = placed[:, :G].astype(bf16)
         filters = jnp.concatenate(
             [filters_of(filt_rows, first + c)[:, :SAMPLES_PAD] for c in range(SUB)], axis=1
@@ -354,7 +357,7 @@
     rounded = exact.astype(jnp.bfloat16)
     remainder = (exact - rounded.astype(np.float32)).astype(jnp.bfloat16)
     table = jnp.asarray(rounded)
-    table_t = jnp.asarray(rounded.T)
+    table_t = jnp.asarray(np.stack([rounded.T, remainder.T]))
     pair_rows = jnp.asarray(np.kron(np.eye(2, dtype=np.float32), rounded.T.astype(np.float32)), jnp.bfloat16)
     split_rows = jnp.asarray(np.concatenate([rounded[:G].T, remainder[:G].T], axis=0))
     columns = jnp.asarray(np.pad(rounded[:G], ((0, 0), (0, -SAMPLES_PAD % LANES))))

time: 75.2 us -> 72 us (0.957)
  Pallas kernels: 52.5 us -> 49.3 us
    pallas_call x2, Pallas kernels: 37.8 us -> 34.5 us  [grid_call(): pl.pallas_call(kernel, grid=(chan_count // GROUP,), in_specs=[grouped(x.s...]
  transfers between devices with their start and end apart: 8 -> 8, of which waited for: 0 -> 0; matrix products, arithmetic and copies ran while one was open for 5% -> 5% of each run, Pallas kernels for 70% -> 69%
where the time goes in v6:
time: 72 us; the launch traced here: 71.7 us
  Pallas kernels  49.3 us (68%)
  starting transfers between devices  14.9 us (21%)
  local copies, waits for them, and re-layouts  3.65 us (5%)
  other arithmetic  3.16 us (4%)
    pallas_call x2, Pallas kernels, grid_call(): pl.pallas_call(kernel, grid=(chan_count // GROUP,), in_specs=[grouped(x.s...  34.5 us
    ppermute x8, starting transfers between devices, passed_along(): return lax.ppermute(value, axis, pairs)  14.9 us
    pallas_call x1, Pallas kernels, sum_call(): pl.pallas_call(sum_kernel, in_specs=[anywhere, anywhere], out_specs=[vmem...  14.7 us
    unnamed x11, local copies, waits for them, and re-layouts  2.03 us
  transfers between devices with their start and end apart: 8, of which 0 were waited for; matrix products, arithmetic and copies ran while one was open for 5% of the time, Pallas kernels for 69%

profile of v6, /device:TPU:0, one launch (start us, length us, event | category | flops | bytes accessed | tf_op | source)
XLA Modules:
  0.0 71.7 jit_solution(15669909626531617630)
XLA Ops:
  0.6 3.1 %collective-permute-start.4 = (bf16[64,16,81]{2,1,0:T(8,128)(2,1)}, bf16[64,16,81]{2,1,0:T(8,128)(2,1)S(1)}, u32[]{:S(2)}, u32[]{:S(2)}) collective-permute-start(bf16[64,16,81]{2,1,0:T(8,128)(2,1)} %bitcast.24), channel_id=1, source_target_pairs={{0,8},{4,12},{8,16},{12,20},{16,24},{20,28},{24,0},{28,4},{1,9},{5... | collective-permute-start | bytes 497672 | tf_op jit(solution)/shard_map/ppermute | solution.py:42
  3.7 1.5 %collective-permute-start.5 = (bf16[64,16,81]{2,1,0:T(8,128)(2,1)}, bf16[64,16,81]{2,1,0:T(8,128)(2,1)S(1)}, u32[]{:S(2)}, u32[]{:S(2)}) collective-permute-start(bf16[64,16,81]{2,1,0:T(8,128)(2,1)} %bitcast.25), channel_id=1, source_target_pairs={{0,4},{4,8},{8,12},{12,16},{16,20},{20,24},{24,28},{28,0},{1,5},{5... | collective-permute-start | bytes 497672 | tf_op jit(solution)/shard_map/ppermute | solution.py:42
  5.2 3.2 %collective-permute-start.6 = (bf16[64,16,81]{2,1,0:T(8,128)(2,1)}, bf16[64,16,81]{2,1,0:T(8,128)(2,1)S(1)}, u32[]{:S(2)}, u32[]{:S(2)}) collective-permute-start(bf16[64,16,81]{2,1,0:T(8,128)(2,1)} %bitcast.26), channel_id=1, source_target_pairs={{0,28},{4,0},{8,4},{12,8},{16,12},{20,16},{24,20},{28,24},{1,29},{... | collective-permute-start | bytes 497672 | tf_op jit(solution)/shard_map/ppermute | solution.py:42
  8.4 0.3 collective-permute-start.7
  8.7 0.7 %iota_compare_fusion = pred[16,32]{1,0:T(8,128)(4,1)S(1)} fusion(s32[16]{0:T(128)} %bitcast.22), kind=kLoop, calls=%fused_computation.5 | loop fusion | flops 512 | bytes 576 | tf_op jit(solution)/shard_map/lt | solution.py:378
  9.5 0.1 lt.40
  9.5 0.8 %reshape_squeeze.3 = s32[1,512]{1,0:T(1,128)S(1)} reshape(s32[1,16,32]{2,1,0:T(8,128)} %param.12) | data formatting | bytes 4096 | tf_op jit(solution)/shard_map/reshape;squeeze | solution.py:374
  10.3 0.6 fusion.1.code_ref
  10.9 17.9 %feature_path.1 = (bf16[64,176,512]{2,1,0:T(8,128)(2,1)}, f32[64,16,81]{2,1,0:T(8,128)}, bf16[64,16,81]{2,1,0:T(8,128)(2,1)}, bf16[64,16,81]{2,1,0:T(8,128)(2,1)...) custom-call(bf16[8,64,81]{2,1,0:T(8,128)(2,1)} %weight_ref.3, bf16[81,64,512]{2,1,0:T(8,128)(2,1)} %bitcast.23, ...), custom_call_target="tpu_custom_call" | custom-call | flops 10240000000 | bytes 16000000 | tf_op jit(solution)/shard_map/feature_path/pallas_call | solution.py:213
  28.8 1.8 %collective-permute-start.3 = (bf16[64,16,81]{2,1,0:T(8,128)(2,1)}, bf16[64,16,81]{2,1,0:T(8,128)(2,1)S(1)}, u32[]{:S(2)}, u32[]{:S(2)}) collective-permute-start(bf16[64,16,81]{2,1,0:T(8,128)(2,1)} %get-tuple-element.17), channel_id=1, source_target_pairs={{0,8},{4,12},{8,16},{12,20},{16,24},{20,28},{24,0},{28,4},{1,9},{5... | collective-permute-start | bytes 497672 | tf_op jit(solution)/shard_map/ppermute | solution.py:42
  30.6 0.0 collective-permute-done.4.refs_0_
  30.6 0.0 collective-permute-start.2
  30.6 4.7 %collective-permute-start.1 = (bf16[64,16,81]{2,1,0:T(8,128)(2,1)}, bf16[64,16,81]{2,1,0:T(8,128)(2,1)S(1)}, u32[]{:S(2)}, u32[]{:S(2)}) collective-permute-start(bf16[64,16,81]{2,1,0:T(8,128)(2,1)} %get-tuple-element.15), channel_id=1, source_target_pairs={{0,28},{4,0},{8,4},{12,8},{16,12},{20,16},{24,20},{28,24},{1,29},{... | collective-permute-start | bytes 497672 | tf_op jit(solution)/shard_map/ppermute | solution.py:42
  35.3 0.0 collective-permute-done.6.refs_3_
  35.3 0.3 collective-permute-start
  35.6 0.0 collective-permute-done.7.refs_4_
  35.6 0.4 copy-done.3
  36.0 0.3 copy-done.4
  36.3 16.6 %filter_path.1 = (f32[8,512]{1,0:T(8,128)}, bf16[512,81]{1,0:T(8,128)(2,1)}) custom-call(bf16[64,176,512]{2,1,0:T(8,128)(2,1)} %get-tuple-element.18.grid_ref, bf16[8,64,81]{2,1,0:T(8,128)(2,1)} %weight_ref.3, s32[1,512]{1,0:T(1,128)} %fusion.1.code_ref, bf16[8,512]{1,0:T(8,128)(2,1)} %bitcast.30, bf16[2,176,96]{2,1,0:T(8,128)(2,1)} %constant.62.clone.table_t_ref, ...), custom_call_target="tpu_custom_call" | custom-call | flops 10240000000 | bytes 16000000 | tf_op jit(solution)/shard_map/filter_path/pallas_call | solution.py:213
  53.0 14.7 %sums.1 = (bf16[16,32,81]{2,1,0:T(8,128)(2,1)}, f32[8,512]{1,0:T(8,128)}) custom-call(bf16[16,32,81]{2,1,0:T(8,128)(2,1)} %bitcast.20, f32[8,512]{1,0:T(8,128)} %get-tuple-element.20.radial_ref), custom_call_target="tpu_custom_call" | custom-call | tf_op jit(solution)/shard_map/sums/pallas_call | solution.py:337
  67.7 0.9 %convert_multiply_fusion = f32[16,32,81]{2,1,0:T(8,128)S(1)} fusion(bf16[16,32,81]{2,1,0:T(8,128)(2,1)} %get-tuple-element.22), kind=kLoop, calls=%fused_computation.2 | loop fusion | flops 82944 | bytes 248832 | tf_op jit(solution)/shard_map/mul | solution.py:443
  68.6 0.8 %copy.16 = f32[64,8,81]{2,0,1:T(8,128)} copy(f32[64,8,81]{2,1,0:T(8,128)S(1)} %bitcast.18) | data formatting | bytes 331776 | tf_op jit(solution)/shard_map/mul | solution.py:443
  69.4 0.9 %add_bitcast_fusion = f32[1,64,81,16]{2,3,1,0:T(8,128)} fusion(bf16[64,16,81]{2,1,0:T(8,128)(2,1)S(1)} %collective-permute-done.3, bf16[64,16,81]{2,1,0:T(8,128)(2,1)S(1)} %collective-permute-done.2, bf16[64,16,81]{2,1,0:T(8,128)(2,1)S(1)} %collective-permute-done.1, f32[64,16,81]{2,1,0:T(8,128)S(1)} %copy-done, bf16[64,16,81]{2,1,0:T(8,128)(2,1)S(1)} %collective-permute-done), kind=kLoop, calls=%fused_computation | loop fusion | flops 663552 | bytes 1327104 | tf_op jit(solution)/shard_map/broadcast_in_dim | solution.py:447
  70.4 1.3 %copy.18 = f32[1,8,512]{2,1,0:T(8,128)} copy(f32[1,8,512]{2,1,0:T(8,128)} %bitcast.21) | data formatting | bytes 32768
  (13 shorter events, 0.0 us)
Async XLA Ops:
  0.6 30.0 %collective-permute-start.4 = (bf16[64,16,81]{2,1,0:T(8,128)(2,1)}, bf16[64,16,81]{2,1,0:T(8,128)(2,1)S(1)}, u32[]{:S(2)}, u32[]{:S(2)}) collective-permute-start(bf16[64,16,81]{2,1,0:T(8,128)(2,1)} %bitcast.24), channel_id=1, source_target_pairs={{0,8},{4,12},{8,16},{12,20},{16,24},{20,28},{24,0},{28,4},{1,9},{5... | collective-permute-start | bytes 497672 | tf_op jit(solution)/shard_map/ppermute | solution.py:42
  3.7 26.9 %collective-permute-start.5 = (bf16[64,16,81]{2,1,0:T(8,128)(2,1)}, bf16[64,16,81]{2,1,0:T(8,128)(2,1)S(1)}, u32[]{:S(2)}, u32[]{:S(2)}) collective-permute-start(bf16[64,16,81]{2,1,0:T(8,128)(2,1)} %bitcast.25), channel_id=1, source_target_pairs={{0,4},{4,8},{8,12},{12,16},{16,20},{20,24},{24,28},{28,0},{1,5},{5... | collective-permute-start | bytes 497672 | tf_op jit(solution)/shard_map/ppermute | solution.py:42
  5.2 30.1 %collective-permute-start.6 = (bf16[64,16,81]{2,1,0:T(8,128)(2,1)}, bf16[64,16,81]{2,1,0:T(8,128)(2,1)S(1)}, u32[]{:S(2)}, u32[]{:S(2)}) collective-permute-start(bf16[64,16,81]{2,1,0:T(8,128)(2,1)} %bitcast.26), channel_id=1, source_target_pairs={{0,28},{4,0},{8,4},{12,8},{16,12},{20,16},{24,20},{28,24},{1,29},{... | collective-permute-start | bytes 497672 | tf_op jit(solution)/shard_map/ppermute | solution.py:42
  8.4 27.2 %collective-permute-start.7 = (bf16[64,16,81]{2,1,0:T(8,128)(2,1)}, bf16[64,16,81]{2,1,0:T(8,128)(2,1)S(1)}, u32[]{:S(2)}, u32[]{:S(2)}) collective-permute-start(bf16[64,16,81]{2,1,0:T(8,128)(2,1)} %bitcast.27), channel_id=1, source_target_pairs={{0,24},{4,28},{8,0},{12,4},{16,8},{20,12},{24,16},{28,20},{1,25},{... | collective-permute-start | bytes 497672 | tf_op jit(solution)/shard_map/ppermute | solution.py:42
  28.8 40.6 %collective-permute-start.3 = (bf16[64,16,81]{2,1,0:T(8,128)(2,1)}, bf16[64,16,81]{2,1,0:T(8,128)(2,1)S(1)}, u32[]{:S(2)}, u32[]{:S(2)}) collective-permute-start(bf16[64,16,81]{2,1,0:T(8,128)(2,1)} %get-tuple-element.17), channel_id=1, source_target_pairs={{0,8},{4,12},{8,16},{12,20},{16,24},{20,28},{24,0},{28,4},{1,9},{5... | collective-permute-start | bytes 497672 | tf_op jit(solution)/shard_map/ppermute | solution.py:42
  30.6 5.0 %copy-start.1 = (bf16[64,16,81]{2,1,0:T(8,128)(2,1)}, bf16[64,16,81]{2,1,0:T(8,128)(2,1)S(1)}, u32[]{:S(2)}) copy-start(bf16[64,16,81]{2,1,0:T(8,128)(2,1)S(1)} %collective-permute-done.4.refs_0_) | copy-start | bytes 497668
  30.6 38.8 %collective-permute-start.2 = (bf16[64,16,81]{2,1,0:T(8,128)(2,1)}, bf16[64,16,81]{2,1,0:T(8,128)(2,1)S(1)}, u32[]{:S(2)}, u32[]{:S(2)}) collective-permute-start(bf16[64,16,81]{2,1,0:T(8,128)(2,1)} %get-tuple-element.16), channel_id=1, source_target_pairs={{0,4},{4,8},{8,12},{12,16},{16,20},{20,24},{24,28},{28,0},{1,5},{5... | collective-permute-start | bytes 497672 | tf_op jit(solution)/shard_map/ppermute | solution.py:42
  30.6 5.0 %copy-start.2 = (bf16[64,16,81]{2,1,0:T(8,128)(2,1)}, bf16[64,16,81]{2,1,0:T(8,128)(2,1)S(1)}, u32[]{:S(2)}) copy-start(bf16[64,16,81]{2,1,0:T(8,128)(2,1)S(1)} %collective-permute-done.5.refs_1_) | copy-start | bytes 497668
  30.6 38.8 %collective-permute-start.1 = (bf16[64,16,81]{2,1,0:T(8,128)(2,1)}, bf16[64,16,81]{2,1,0:T(8,128)(2,1)S(1)}, u32[]{:S(2)}, u32[]{:S(2)}) collective-permute-start(bf16[64,16,81]{2,1,0:T(8,128)(2,1)} %get-tuple-element.15), channel_id=1, source_target_pairs={{0,28},{4,0},{8,4},{12,8},{16,12},{20,16},{24,20},{28,24},{1,29},{... | collective-permute-start | bytes 497672 | tf_op jit(solution)/shard_map/ppermute | solution.py:42
  35.3 0.7 %copy-start.3 = (bf16[64,16,81]{2,1,0:T(8,128)(2,1)}, bf16[64,16,81]{2,1,0:T(8,128)(2,1)S(1)}, u32[]{:S(2)}) copy-start(bf16[64,16,81]{2,1,0:T(8,128)(2,1)S(1)} %collective-permute-done.6.refs_3_) | copy-start | bytes 497668
  35.3 34.1 %collective-permute-start = (bf16[64,16,81]{2,1,0:T(8,128)(2,1)}, bf16[64,16,81]{2,1,0:T(8,128)(2,1)S(1)}, u32[]{:S(2)}, u32[]{:S(2)}) collective-permute-start(bf16[64,16,81]{2,1,0:T(8,128)(2,1)} %get-tuple-element.14), channel_id=1, source_target_pairs={{0,24},{4,28},{8,0},{12,4},{16,8},{20,12},{24,16},{28,20},{1,25},{... | collective-permute-start | bytes 497672 | tf_op jit(solution)/shard_map/ppermute | solution.py:42
  35.6 0.7 copy-start.4
  36.3 33.1 %copy-start = (f32[64,16,81]{2,1,0:T(8,128)S(1)}, f32[64,16,81]{2,1,0:T(8,128)}, u32[]{:S(2)}) copy-start(f32[64,16,81]{2,1,0:T(8,128)} %get-tuple-element.13) | copy-start | bytes 995332

commit v7 on v6

--- a/solution.py
+++ b/solution.py
@@ -319,7 +319,7 @@
     radial_total = slots[0]
     for index in range(1, chans):
         radial_total = radial_total + slots[index]
-    radial_out[...] = radial_total * (1.0 / SAMPLES)
+    radial_out[...] = radial_total
 
     @pl.loop(1, count)
     def _(step):
@@ -371,12 +371,12 @@
         own_block if offset == 0 else passed_along(own_block, "atom", -offset)
         for offset in offsets
     ]
-    sources = neighbors[0].reshape(-1)
+    sources = neighbors[0]
     slot_index = (
         sources // block_len - position + REACH
     ) % atom_count * block_len + sources % block_len
-    valid = (jnp.arange(SLOTS, dtype=jnp.int32)[None, :] < counts[0][:, None]).reshape(-1)
-    code = jnp.where(valid, slot_index, -1)[None, :]
+    valid = (jnp.arange(SLOTS, dtype=jnp.int32)[None, :] < counts[0][:, None])
+    code = jnp.where(valid, slot_index, -1).reshape(1, -1)
     radial_e = radial[0]
     basis_count = radial_e.shape[0]
     edges = radial_e.shape[1]
@@ -445,7 +445,7 @@
     for block in arrived:
         returned_sum = returned_sum + block.astype(jnp.float32)
     feat_grad = jnp.transpose(returned_sum, (0, 2, 1))[None]
-    return (feat_grad, radial_grad[None], weight_grad)
+    return (feat_grad, radial_grad[None] * (1.0 / SAMPLES), weight_grad)
 
 
 def solution(mesh):

time: 72 us -> 72 us (level)
  other arithmetic: 3.16 us -> 4.49 us
  local copies, waits for them, and re-layouts: 3.65 us -> 2.33 us
    mul x0 -> x1, other arithmetic: none -> 1.32 us  [local(): return (feat_grad, radial_grad[None] * (1.0 / SAMPLES), weight_grad)]
    unnamed x11 -> x10, local copies, waits for them, and re-layouts: 2.03 us -> 0.71 us
    another operation x1 -> x0, local copies, waits for them, and re-layouts: 0.78 us -> none  [local(): sources = neighbors[0].reshape(-1)]
    squeeze x0 -> x1, local copies, waits for them, and re-layouts: none -> 0.78 us  [local(): sources = neighbors[0]]
  transfers between devices with their start and end apart: 8 -> 8, of which waited for: 0 -> 0; matrix products, arithmetic and copies ran while one was open for 5% -> 7% of each run, Pallas kernels for 69% -> 69%
where the time goes in v7:
time: 72 us; the launch traced here: 71.7 us
  Pallas kernels  49.3 us (68%)
  starting transfers between devices  14.9 us (21%)
  other arithmetic  4.49 us (6%)
  local copies, waits for them, and re-layouts  2.33 us (3%)
    pallas_call x2, Pallas kernels, grid_call(): pl.pallas_call(kernel, grid=(chan_count // GROUP,), in_specs=[grouped(x.s...  34.5 us
    ppermute x8, starting transfers between devices, passed_along(): return lax.ppermute(value, axis, pairs)  14.9 us
    pallas_call x1, Pallas kernels, sum_call(): pl.pallas_call(sum_kernel, in_specs=[anywhere, anywhere], out_specs=[vmem...  14.7 us
  transfers between devices with their start and end apart: 8, of which 0 were waited for; matrix products, arithmetic and copies ran while one was open for 7% of the time, Pallas kernels for 69%

profile of v7, /device:TPU:0, one launch (start us, length us, event | category | flops | bytes accessed | tf_op | source)
XLA Modules:
  0.0 71.7 jit_solution(3733854127200925613)
XLA Ops:
  0.6 3.1 %collective-permute-start.4 = (bf16[64,16,81]{2,1,0:T(8,128)(2,1)}, bf16[64,16,81]{2,1,0:T(8,128)(2,1)S(1)}, u32[]{:S(2)}, u32[]{:S(2)}) collective-permute-start(bf16[64,16,81]{2,1,0:T(8,128)(2,1)} %bitcast.24), channel_id=1, source_target_pairs={{0,8},{4,12},{8,16},{12,20},{16,24},{20,28},{24,0},{28,4},{1,9},{5... | collective-permute-start | bytes 497672 | tf_op jit(solution)/shard_map/ppermute | solution.py:42
  3.7 1.5 %collective-permute-start.5 = (bf16[64,16,81]{2,1,0:T(8,128)(2,1)}, bf16[64,16,81]{2,1,0:T(8,128)(2,1)S(1)}, u32[]{:S(2)}, u32[]{:S(2)}) collective-permute-start(bf16[64,16,81]{2,1,0:T(8,128)(2,1)} %bitcast.25), channel_id=1, source_target_pairs={{0,4},{4,8},{8,12},{12,16},{16,20},{20,24},{24,28},{28,0},{1,5},{5... | collective-permute-start | bytes 497672 | tf_op jit(solution)/shard_map/ppermute | solution.py:42
  5.2 3.2 %collective-permute-start.6 = (bf16[64,16,81]{2,1,0:T(8,128)(2,1)}, bf16[64,16,81]{2,1,0:T(8,128)(2,1)S(1)}, u32[]{:S(2)}, u32[]{:S(2)}) collective-permute-start(bf16[64,16,81]{2,1,0:T(8,128)(2,1)} %bitcast.26), channel_id=1, source_target_pairs={{0,28},{4,0},{8,4},{12,8},{16,12},{20,16},{24,20},{28,24},{1,29},{... | collective-permute-start | bytes 497672 | tf_op jit(solution)/shard_map/ppermute | solution.py:42
  8.4 0.3 collective-permute-start.7
  8.7 0.7 %iota_compare_fusion = pred[16,32]{1,0:T(8,128)(4,1)S(1)} fusion(s32[16]{0:T(128)} %bitcast.22), kind=kLoop, calls=%fused_computation.6 | loop fusion | flops 512 | bytes 576 | tf_op jit(solution)/shard_map/lt | solution.py:378
  9.5 0.1 lt.39
  9.5 0.8 %squeeze.13 = s32[1,512]{1,0:T(1,128)S(1)} reshape(s32[1,16,32]{2,1,0:T(8,128)} %param.12) | data formatting | bytes 4096 | tf_op jit(solution)/shard_map/squeeze | solution.py:374
  10.3 0.6 fusion.1.code_ref
  10.9 17.9 %feature_path.1 = (bf16[64,176,512]{2,1,0:T(8,128)(2,1)}, f32[64,16,81]{2,1,0:T(8,128)}, bf16[64,16,81]{2,1,0:T(8,128)(2,1)}, bf16[64,16,81]{2,1,0:T(8,128)(2,1)...) custom-call(bf16[8,64,81]{2,1,0:T(8,128)(2,1)} %weight_ref.3, bf16[81,64,512]{2,1,0:T(8,128)(2,1)} %bitcast.23, ...), custom_call_target="tpu_custom_call" | custom-call | flops 10240000000 | bytes 16000000 | tf_op jit(solution)/shard_map/feature_path/pallas_call | solution.py:213
  28.8 1.8 %collective-permute-start.3 = (bf16[64,16,81]{2,1,0:T(8,128)(2,1)}, bf16[64,16,81]{2,1,0:T(8,128)(2,1)S(1)}, u32[]{:S(2)}, u32[]{:S(2)}) collective-permute-start(bf16[64,16,81]{2,1,0:T(8,128)(2,1)} %get-tuple-element.17), channel_id=1, source_target_pairs={{0,8},{4,12},{8,16},{12,20},{16,24},{20,28},{24,0},{28,4},{1,9},{5... | collective-permute-start | bytes 497672 | tf_op jit(solution)/shard_map/ppermute | solution.py:42
  30.6 0.0 collective-permute-done.4.refs_0_
  30.6 0.0 collective-permute-start.2
  30.6 4.7 %collective-permute-start.1 = (bf16[64,16,81]{2,1,0:T(8,128)(2,1)}, bf16[64,16,81]{2,1,0:T(8,128)(2,1)S(1)}, u32[]{:S(2)}, u32[]{:S(2)}) collective-permute-start(bf16[64,16,81]{2,1,0:T(8,128)(2,1)} %get-tuple-element.15), channel_id=1, source_target_pairs={{0,28},{4,0},{8,4},{12,8},{16,12},{20,16},{24,20},{28,24},{1,29},{... | collective-permute-start | bytes 497672 | tf_op jit(solution)/shard_map/ppermute | solution.py:42
  35.3 0.0 collective-permute-done.6.refs_3_
  35.3 0.3 collective-permute-start
  35.6 0.0 collective-permute-done.7.refs_4_
  35.6 0.4 copy-done.3
  36.0 0.3 copy-done.4
  36.3 16.6 %filter_path.1 = (f32[8,512]{1,0:T(8,128)}, bf16[512,81]{1,0:T(8,128)(2,1)}) custom-call(bf16[64,176,512]{2,1,0:T(8,128)(2,1)} %get-tuple-element.18.grid_ref, bf16[8,64,81]{2,1,0:T(8,128)(2,1)} %weight_ref.3, s32[1,512]{1,0:T(1,128)} %fusion.1.code_ref, bf16[8,512]{1,0:T(8,128)(2,1)} %bitcast.30, bf16[2,176,96]{2,1,0:T(8,128)(2,1)} %constant.64.clone.table_t_ref, ...), custom_call_target="tpu_custom_call" | custom-call | flops 10240000000 | bytes 16000000 | tf_op jit(solution)/shard_map/filter_path/pallas_call | solution.py:213
  53.0 14.7 %sums.1 = (bf16[16,32,81]{2,1,0:T(8,128)(2,1)}, f32[8,512]{1,0:T(8,128)}) custom-call(bf16[16,32,81]{2,1,0:T(8,128)(2,1)} %bitcast.21, f32[8,512]{1,0:T(8,128)} %get-tuple-element.20.radial_ref), custom_call_target="tpu_custom_call" | custom-call | tf_op jit(solution)/shard_map/sums/pallas_call | solution.py:337
  67.7 0.9 %convert_multiply_fusion = f32[16,32,81]{2,1,0:T(8,128)S(1)} fusion(bf16[16,32,81]{2,1,0:T(8,128)(2,1)} %get-tuple-element.22), kind=kLoop, calls=%fused_computation.2 | loop fusion | flops 82944 | bytes 248832 | tf_op jit(solution)/shard_map/mul | solution.py:443
  68.6 0.8 %copy.16 = f32[64,8,81]{2,0,1:T(8,128)} copy(f32[64,8,81]{2,1,0:T(8,128)S(1)} %bitcast.19) | data formatting | bytes 331776 | tf_op jit(solution)/shard_map/mul | solution.py:443
  69.4 1.3 %multiply_bitcast_fusion = f32[1,8,512]{2,1,0:T(8,128)} fusion(f32[8,512]{1,0:T(8,128)} %get-tuple-element.21), kind=kLoop, calls=%fused_computation.3 | loop fusion | flops 4096 | bytes 32768 | tf_op jit(solution)/shard_map/mul | solution.py:448
  70.8 0.9 %add_bitcast_fusion = f32[1,64,81,16]{2,3,1,0:T(8,128)} fusion(bf16[64,16,81]{2,1,0:T(8,128)(2,1)S(1)} %collective-permute-done.3, bf16[64,16,81]{2,1,0:T(8,128)(2,1)S(1)} %collective-permute-done.2, bf16[64,16,81]{2,1,0:T(8,128)(2,1)S(1)} %collective-permute-done.1, f32[64,16,81]{2,1,0:T(8,128)S(1)} %copy-done, bf16[64,16,81]{2,1,0:T(8,128)(2,1)S(1)} %collective-permute-done), kind=kLoop, calls=%fused_computation | loop fusion | flops 663552 | bytes 1327104 | tf_op jit(solution)/shard_map/broadcast_in_dim | solution.py:447
  (13 shorter events, 0.0 us)
Async XLA Ops:
  0.6 30.0 %collective-permute-start.4 = (bf16[64,16,81]{2,1,0:T(8,128)(2,1)}, bf16[64,16,81]{2,1,0:T(8,128)(2,1)S(1)}, u32[]{:S(2)}, u32[]{:S(2)}) collective-permute-start(bf16[64,16,81]{2,1,0:T(8,128)(2,1)} %bitcast.24), channel_id=1, source_target_pairs={{0,8},{4,12},{8,16},{12,20},{16,24},{20,28},{24,0},{28,4},{1,9},{5... | collective-permute-start | bytes 497672 | tf_op jit(solution)/shard_map/ppermute | solution.py:42
  3.7 26.9 %collective-permute-start.5 = (bf16[64,16,81]{2,1,0:T(8,128)(2,1)}, bf16[64,16,81]{2,1,0:T(8,128)(2,1)S(1)}, u32[]{:S(2)}, u32[]{:S(2)}) collective-permute-start(bf16[64,16,81]{2,1,0:T(8,128)(2,1)} %bitcast.25), channel_id=1, source_target_pairs={{0,4},{4,8},{8,12},{12,16},{16,20},{20,24},{24,28},{28,0},{1,5},{5... | collective-permute-start | bytes 497672 | tf_op jit(solution)/shard_map/ppermute | solution.py:42
  5.2 30.1 %collective-permute-start.6 = (bf16[64,16,81]{2,1,0:T(8,128)(2,1)}, bf16[64,16,81]{2,1,0:T(8,128)(2,1)S(1)}, u32[]{:S(2)}, u32[]{:S(2)}) collective-permute-start(bf16[64,16,81]{2,1,0:T(8,128)(2,1)} %bitcast.26), channel_id=1, source_target_pairs={{0,28},{4,0},{8,4},{12,8},{16,12},{20,16},{24,20},{28,24},{1,29},{... | collective-permute-start | bytes 497672 | tf_op jit(solution)/shard_map/ppermute | solution.py:42
  8.4 27.2 %collective-permute-start.7 = (bf16[64,16,81]{2,1,0:T(8,128)(2,1)}, bf16[64,16,81]{2,1,0:T(8,128)(2,1)S(1)}, u32[]{:S(2)}, u32[]{:S(2)}) collective-permute-start(bf16[64,16,81]{2,1,0:T(8,128)(2,1)} %bitcast.27), channel_id=1, source_target_pairs={{0,24},{4,28},{8,0},{12,4},{16,8},{20,12},{24,16},{28,20},{1,25},{... | collective-permute-start | bytes 497672 | tf_op jit(solution)/shard_map/ppermute | solution.py:42
  28.8 41.9 %collective-permute-start.3 = (bf16[64,16,81]{2,1,0:T(8,128)(2,1)}, bf16[64,16,81]{2,1,0:T(8,128)(2,1)S(1)}, u32[]{:S(2)}, u32[]{:S(2)}) collective-permute-start(bf16[64,16,81]{2,1,0:T(8,128)(2,1)} %get-tuple-element.17), channel_id=1, source_target_pairs={{0,8},{4,12},{8,16},{12,20},{16,24},{20,28},{24,0},{28,4},{1,9},{5... | collective-permute-start | bytes 497672 | tf_op jit(solution)/shard_map/ppermute | solution.py:42
  30.6 5.0 %copy-start.1 = (bf16[64,16,81]{2,1,0:T(8,128)(2,1)}, bf16[64,16,81]{2,1,0:T(8,128)(2,1)S(1)}, u32[]{:S(2)}) copy-start(bf16[64,16,81]{2,1,0:T(8,128)(2,1)S(1)} %collective-permute-done.4.refs_0_) | copy-start | bytes 497668
  30.6 40.1 %collective-permute-start.2 = (bf16[64,16,81]{2,1,0:T(8,128)(2,1)}, bf16[64,16,81]{2,1,0:T(8,128)(2,1)S(1)}, u32[]{:S(2)}, u32[]{:S(2)}) collective-permute-start(bf16[64,16,81]{2,1,0:T(8,128)(2,1)} %get-tuple-element.16), channel_id=1, source_target_pairs={{0,4},{4,8},{8,12},{12,16},{16,20},{20,24},{24,28},{28,0},{1,5},{5... | collective-permute-start | bytes 497672 | tf_op jit(solution)/shard_map/ppermute | solution.py:42
  30.6 5.0 %copy-start.2 = (bf16[64,16,81]{2,1,0:T(8,128)(2,1)}, bf16[64,16,81]{2,1,0:T(8,128)(2,1)S(1)}, u32[]{:S(2)}) copy-start(bf16[64,16,81]{2,1,0:T(8,128)(2,1)S(1)} %collective-permute-done.5.refs_1_) | copy-start | bytes 497668
  30.6 40.1 %collective-permute-start.1 = (bf16[64,16,81]{2,1,0:T(8,128)(2,1)}, bf16[64,16,81]{2,1,0:T(8,128)(2,1)S(1)}, u32[]{:S(2)}, u32[]{:S(2)}) collective-permute-start(bf16[64,16,81]{2,1,0:T(8,128)(2,1)} %get-tuple-element.15), channel_id=1, source_target_pairs={{0,28},{4,0},{8,4},{12,8},{16,12},{20,16},{24,20},{28,24},{1,29},{... | collective-permute-start | bytes 497672 | tf_op jit(solution)/shard_map/ppermute | solution.py:42
  35.3 0.7 %copy-start.3 = (bf16[64,16,81]{2,1,0:T(8,128)(2,1)}, bf16[64,16,81]{2,1,0:T(8,128)(2,1)S(1)}, u32[]{:S(2)}) copy-start(bf16[64,16,81]{2,1,0:T(8,128)(2,1)S(1)} %collective-permute-done.6.refs_3_) | copy-start | bytes 497668
  35.3 35.4 %collective-permute-start = (bf16[64,16,81]{2,1,0:T(8,128)(2,1)}, bf16[64,16,81]{2,1,0:T(8,128)(2,1)S(1)}, u32[]{:S(2)}, u32[]{:S(2)}) collective-permute-start(bf16[64,16,81]{2,1,0:T(8,128)(2,1)} %get-tuple-element.14), channel_id=1, source_target_pairs={{0,24},{4,28},{8,0},{12,4},{16,8},{20,12},{24,16},{28,20},{1,25},{... | collective-permute-start | bytes 497672 | tf_op jit(solution)/shard_map/ppermute | solution.py:42
  35.6 0.7 copy-start.4
  36.3 34.4 %copy-start = (f32[64,16,81]{2,1,0:T(8,128)S(1)}, f32[64,16,81]{2,1,0:T(8,128)}, u32[]{:S(2)}) copy-start(f32[64,16,81]{2,1,0:T(8,128)} %get-tuple-element.13) | copy-start | bytes 995332
